TPU v7x, 512 devices: a whole 4x4x16 slice. The times are simulated.
512 devices in a mesh: mode: 16 (over y, x), rest: 32 (over z, core).
Axes of the slice: x: 4, y: 4, z: 16, core: 2. Of those that a mesh axis runs over, the one named last changes fastest.
Arguments:
- unfolded: bfloat16 [1024, 131072], P('mode', 'rest'), as said below
- initial: float32 [1024, 128], P('mode'), may hold values from -6 to 6
Outputs:
- basis: float32 [1024, 128], P('mode')
- core: float32 [128, 131072], P('mode', 'rest')
Inputs may be any that keep to these rules, and one draw needn't show every extreme that they name: `unfolded`: entries are bounded, with row and column scales that differ.
All inputs are finite; a program needn't handle non-finite values.
Results may differ from a plain program's by a relative error of at most 0.0029.
Values may be sent and summed in bfloat16 or wider, within the bound.
No kernel may reach another device: no remote copies, remote signals or barrier semaphores. Data moves between devices by JAX's collectives and lax.ppermute only.
A program may use at most 64 MiB of HBM per device.

v0:
```python
import jax
import jax.numpy as jnp
from jax import lax
from jax.sharding import PartitionSpec as P

ITERS = 4


def on_device(unfolded, initial):
    columns = unfolded.shape[1] * lax.axis_size("rest")
    slab = lax.all_gather(unfolded, "mode", axis=0, tiled=True)
    partial_value = lax.dot_general(
        unfolded, slab, (((1,), (1,)), ((), ())), preferred_element_type=jnp.float32
    )
    gram_rows = lax.psum(partial_value, "rest") / columns
    basis = initial
    for sweep in range(ITERS):
        whole_basis = lax.all_gather(basis, "mode", axis=0, tiled=True)
        image = jnp.dot(gram_rows, whole_basis, precision=lax.Precision.HIGHEST)
        correlation = lax.psum(jnp.dot(image.T, image, precision=lax.Precision.HIGHEST), "mode")
        factor = jnp.linalg.cholesky(correlation)
        basis = jax.scipy.linalg.solve_triangular(factor, image.T, lower=True).T
    basis_half = basis.astype(jnp.bfloat16)
    full_cols = lax.all_to_all(basis_half, "mode", split_axis=1, concat_axis=0, tiled=True)
    core = lax.dot_general(
        full_cols, slab, (((0,), (0,)), ((), ())), preferred_element_type=jnp.float32
    )
    return (basis, core)


def solution(mesh):
    in_specs = (P("mode", "rest"), P("mode", None))
    out_specs = (P("mode", None), P("mode", "rest"))
    return jax.shard_map(
        on_device, mesh=mesh, in_specs=in_specs, out_specs=out_specs, check_vma=False
    )
```

profile of v0, /device:TPU:1, one launch (start us, length us, event | category | flops | bytes accessed | tf_op | source)
XLA Modules:
  0.0 961.2 jit_solution(15461624391746891040)
XLA Ops:
  7.2 0.7 all-gather.2.cloned.1.call-update
  8.0 94.5 %all-gather.2.cloned.1.call-done = bf16[1024,4096]{1,0:T(8,128)(2,1)} async-done(((bf16[64,4096]{1,0:T(8,128)(2,1)}), bf16[1024,4096]{1,0:T(8,128)(2,1)}) %all-gather.2.cloned.1.call-update) | async-done | bytes 8388624 | tf_op jit(solution)/shard_map/all_gather | solution.py:11
  102.4 6.9 fusion.39
  109.4 18.1 %all_gather.16 = f32[1024,128]{1,0:T(8,128)S(1)} all-gather(f32[64,128]{1,0:T(8,128)S(1)} %copy-done), channel_id=1, replica_groups=mesh['mode'=16,'rest'=32] {'mode'}, dimensions={0}, use_global_device_ids=true | all-gather | bytes 557056 | tf_op jit(solution)/shard_map/all_gather | solution.py:18
  127.5 188.0 %all-reduce.6.cloned.1.call-done = f32[64,1024]{1,0:T(8,128)} async-done(((f32[64,1024]{1,0:T(8,128)}), f32[64,1024]{1,0:T(8,128)}) %all-reduce.6.cloned.1.call-update) | async-done | bytes 262160 | tf_op jit(solution)/shard_map/psum | solution.py:15
  315.5 1.4 fusion.6
  316.9 0.9 fusion.40
  317.9 111.5 %all-reduce.8.cloned.1.call-done = f32[128,128]{0,1:T(8,128)} async-done(((f32[128,128]{0,1:T(8,128)}), f32[128,128]{0,1:T(8,128)}) %all-reduce.8.cloned.1.call-update) | async-done | bytes 65552 | tf_op jit(solution)/shard_map/psum | solution.py:20
  429.4 0.9 copy.23
  430.4 0.9 fusion.23
  431.2 11.7 %cholesky.74 = f32[128,128]{1,0:T(8,128)S(1)} custom-call(f32[128,128]{1,0:T(8,128)S(1)} %fusion.23), custom_call_target="Cholesky" | custom-call | tf_op jit(solution)/shard_map/jit(cholesky)/cholesky | solution.py:21
  443.0 0.6 compare_reduce_fusion.3
  443.6 0.7 fusion.12
  444.3 9.8 %custom-call.8 = f32[1,128,128]{1,2,0:T(8,128)S(1)} custom-call(f32[1,128,128]{2,1,0:T(8,128)S(1)} %fusion.12), custom_call_target="InvertDiagBlocksLowerTriangular" | custom-call | tf_op jit(solution)/shard_map/jit(_solve_triangular)/triangular_solve | solution.py:22
  454.3 17.8 %all_gather.17 = f32[1024,128]{1,0:T(8,128)S(1)} all-gather(f32[64,128]{1,0:T(8,128)S(1)} %convolution_bitcast_fusion.3), channel_id=1, replica_groups=mesh['mode'=16,'rest'=32] {'mode'}, dimensions={0}, use_global_device_ids=true | all-gather | bytes 557056 | tf_op jit(solution)/shard_map/all_gather | solution.py:18
  472.1 1.4 fusion.4
  473.4 0.9 fusion.41
  474.6 115.7 %all-reduce.10.cloned.1.call-done = f32[128,128]{0,1:T(8,128)} async-done(((f32[128,128]{0,1:T(8,128)}), f32[128,128]{0,1:T(8,128)}) %all-reduce.10.cloned.1.call-update) | async-done | bytes 65552 | tf_op jit(solution)/shard_map/psum | solution.py:20
  590.4 0.9 copy.25
  591.3 0.9 fusion.21
  592.1 11.7 %cholesky.85 = f32[128,128]{1,0:T(8,128)S(1)} custom-call(f32[128,128]{1,0:T(8,128)S(1)} %fusion.21), custom_call_target="Cholesky" | custom-call | tf_op jit(solution)/shard_map/jit(cholesky)/cholesky | solution.py:21
  603.9 0.6 compare_reduce_fusion.2
  604.5 0.7 fusion.13
  605.2 9.8 %custom-call.9 = f32[1,128,128]{1,2,0:T(8,128)S(1)} custom-call(f32[1,128,128]{2,1,0:T(8,128)S(1)} %fusion.13), custom_call_target="InvertDiagBlocksLowerTriangular" | custom-call | tf_op jit(solution)/shard_map/jit(_solve_triangular)/triangular_solve | solution.py:22
  615.2 17.8 %all_gather.18 = f32[1024,128]{1,0:T(8,128)S(1)} all-gather(f32[64,128]{1,0:T(8,128)S(1)} %convolution_bitcast_fusion.2), channel_id=1, replica_groups=mesh['mode'=16,'rest'=32] {'mode'}, dimensions={0}, use_global_device_ids=true | all-gather | bytes 557056 | tf_op jit(solution)/shard_map/all_gather | solution.py:18
  633.0 1.4 fusion.2
  634.4 0.9 fusion.42
  635.3 0.3 all-reduce.14.cloned.1.call-start
  635.6 115.7 %all-reduce.12.cloned.1.call-done = f32[128,128]{0,1:T(8,128)} async-done(((f32[128,128]{0,1:T(8,128)}), f32[128,128]{0,1:T(8,128)}) %all-reduce.12.cloned.1.call-update) | async-done | bytes 65552 | tf_op jit(solution)/shard_map/psum | solution.py:20
  751.2 0.9 copy.27
  752.2 0.9 fusion.19
  753.0 11.7 %cholesky.96 = f32[128,128]{1,0:T(8,128)S(1)} custom-call(f32[128,128]{1,0:T(8,128)S(1)} %fusion.19), custom_call_target="Cholesky" | custom-call | tf_op jit(solution)/shard_map/jit(cholesky)/cholesky | solution.py:21
  764.8 0.6 compare_reduce_fusion.1
  765.4 0.7 fusion.14
  766.1 9.8 %custom-call.10 = f32[1,128,128]{1,2,0:T(8,128)S(1)} custom-call(f32[1,128,128]{2,1,0:T(8,128)S(1)} %fusion.14), custom_call_target="InvertDiagBlocksLowerTriangular" | custom-call | tf_op jit(solution)/shard_map/jit(_solve_triangular)/triangular_solve | solution.py:22
  776.1 18.0 %all_gather.19 = f32[1024,128]{1,0:T(8,128)S(1)} all-gather(f32[64,128]{1,0:T(8,128)S(1)} %convolution_bitcast_fusion.1), channel_id=1, replica_groups=mesh['mode'=16,'rest'=32] {'mode'}, dimensions={0}, use_global_device_ids=true | all-gather | bytes 557056 | tf_op jit(solution)/shard_map/all_gather | solution.py:18
  794.1 1.4 fusion
  795.5 0.9 fusion.43
  796.5 116.0 %all-reduce.14.cloned.1.call-done = f32[128,128]{0,1:T(8,128)} async-done(((f32[128,128]{0,1:T(8,128)}), f32[128,128]{0,1:T(8,128)}) %all-reduce.14.cloned.1.call-update) | async-done | bytes 65552 | tf_op jit(solution)/shard_map/psum | solution.py:20
  912.4 0.9 copy.29
  913.4 0.9 fusion.17
  914.2 11.7 %cholesky.107 = f32[128,128]{1,0:T(8,128)S(1)} custom-call(f32[128,128]{1,0:T(8,128)S(1)} %fusion.17), custom_call_target="Cholesky" | custom-call | tf_op jit(solution)/shard_map/jit(cholesky)/cholesky | solution.py:21
  926.0 0.6 compare_reduce_fusion
  926.6 0.7 fusion.15
  927.3 9.8 %custom-call.11 = f32[1,128,128]{1,2,0:T(8,128)S(1)} custom-call(f32[1,128,128]{2,1,0:T(8,128)S(1)} %fusion.15), custom_call_target="InvertDiagBlocksLowerTriangular" | custom-call | tf_op jit(solution)/shard_map/jit(_solve_triangular)/triangular_solve | solution.py:22
  937.1 0.8 fusion.38
  938.1 10.8 %all_to_all.19 = bf16[16,2,256]{2,1,0:T(2,128)(2,1)S(1)} all-to-all(bf16[16,2,256]{2,1,0:T(2,128)(2,1)S(1)} %reshape.15), channel_id=1, replica_groups=mesh['mode'=16,'rest'=32] {'mode'}, dimensions={0} | all-to-all | bytes 32768 | tf_op jit(solution)/shard_map/all_to_all | solution.py:24
  949.1 5.2 fusion.44
  (26 shorter events, 1.6 us)
Async XLA Ops:
  7.2 102.3 %copy-start = (f32[64,128]{1,0:T(8,128)S(1)}, f32[64,128]{1,0:T(8,128)}, u32[]{:S(2)}) copy-start(f32[64,128]{1,0:T(8,128)} %param.6) | copy-start | bytes 98308
  7.2 95.2 %all-gather.2.cloned.1.call-start = ((), (), s32[]{:S(2)}) async-start(), calls=%async_computation.1 | async-start | bytes 8912896 | tf_op jit(solution)/shard_map/all_gather | solution.py:11
  7.9 307.6 %all-reduce.6.cloned.1.call-start = ((), (), s32[]{:S(2)}) async-start(), calls=%async_computation.2 | async-start | bytes 524288 | tf_op jit(solution)/shard_map/psum | solution.py:15
  109.4 320.1 %all-reduce.8.cloned.1.call-start = ((), (), s32[]{:S(2)}) async-start(), calls=%async_computation.3 | async-start | bytes 131072 | tf_op jit(solution)/shard_map/psum | solution.py:20
  317.9 272.5 %all-reduce.10.cloned.1.call-start = ((), (), s32[]{:S(2)}) async-start(), calls=%async_computation.4 | async-start | bytes 131072 | tf_op jit(solution)/shard_map/psum | solution.py:20
  474.4 276.9 %all-reduce.12.cloned.1.call-start = ((), (), s32[]{:S(2)}) async-start(), calls=%async_computation.5 | async-start | bytes 131072 | tf_op jit(solution)/shard_map/psum | solution.py:20
  635.3 277.1 %all-reduce.14.cloned.1.call-start = ((), (), s32[]{:S(2)}) async-start(), calls=%async_computation.6 | async-start | bytes 131072 | tf_op jit(solution)/shard_map/psum | solution.py:20
Sparse Core Ops, SparseCore 0:
  11.0 91.3 all-gather.1
  109.5 205.9 all-reduce.5
  319.6 109.7 all-reduce.7
  474.5 115.7 all-reduce.9
  635.4 115.7 all-reduce.11
  796.6 115.7 all-reduce.13
where the time goes:
time: 964 us; the launch traced here: 961 us
  waiting for transfers between devices  742 us (77%)
  other arithmetic  94.8 us (10%)
  blocking collectives  82.4 us (9%)
  matrix products  22.8 us (2%)
  between operations  14.3 us (1%)
    psum x4, waiting for transfers between devices, on_device(): lax.psum(jnp.dot(image.T, image, precision=lax.Precision.HIGHEST), 'mode')  459 us
    psum x1, waiting for transfers between devices, on_device(): gram_rows = lax.psum(partial_value, 'rest') / columns  188 us
    all_gather x1, waiting for transfers between devices, on_device(): slab = lax.all_gather(unfolded, 'mode', axis=0, tiled=True)  94.5 us
    all_gather x4, blocking collectives, on_device(): whole_basis = lax.all_gather(basis, 'mode', axis=0, tiled=True)  71.7 us
    another operation x12, other arithmetic, on_device(): factor = jnp.linalg.cholesky(correlation)  49.6 us
    another operation x8, other arithmetic, on_device(): basis = jax.scipy.linalg.solve_triangular(factor, image.T, lower=True).T  41.9 us
  transfers between devices with their start and end apart: 6, of which 6 were waited for; matrix products, arithmetic and copies ran while one was open for 0% of the time, Pallas kernels for 0%

commit v1 on v0

v1 whole, which is shorter than its diff:
```python
import jax
import jax.numpy as jnp
from jax import lax
from jax.experimental import pallas as pl
from jax.experimental.pallas import tpu as pltpu
from jax.sharding import Mesh, PartitionSpec as P

ITERS = 4
ROWS = 1024
RANK = 128
BLOCK = 128
HALF_BLOCKS = 18
SPLIT = 16
SLIVER = BLOCK // SPLIT
LEAST_PIVOT = 2e-3
MODE = ("y", "x")

SLOTS = [(t, t + d) for t in range(4) for d in range(4)]


def split_two(value):
    high = value.astype(jnp.bfloat16)
    return high, (value - high.astype(jnp.float32)).astype(jnp.bfloat16)


def dot_nt(left, right):
    return lax.dot_general(left, right, (((1,), (1,)), ((), ())), preferred_element_type=jnp.float32)


def dot_tn(left, right):
    return lax.dot_general(left, right, (((0,), (0,)), ((), ())), preferred_element_type=jnp.float32)


def dot_nn(left, right):
    return jnp.dot(left, right, preferred_element_type=jnp.float32)


def gram_kernel(place_ref, own_ref, twin_ref, out_ref):
    core = place_ref[0]

    def rows(ref, a):
        start = pl.multiple_of(lax.rem(core * 512 + a * 256, ROWS), 256)
        return ref[pl.ds(start, 256), :]

    own = [rows(own_ref, a) for a in range(4)]
    twin = [rows(twin_ref, a) for a in range(4)]
    tiles = {}
    for a, b in ((0, 0), (0, 1), (0, 2), (1, 1), (1, 2), (1, 3)):
        tiles[a, b] = dot_nt(own[a], own[b]) + dot_nt(twin[a], twin[b])

    def block(a, b):
        tile = tiles[a // 2, b // 2]
        return tile[(a % 2) * BLOCK : (a % 2 + 1) * BLOCK, (b % 2) * BLOCK : (b % 2 + 1) * BLOCK]

    for slot, (a, b) in enumerate(SLOTS):
        out_ref[:, slot] = block(a, b).reshape(SPLIT, SLIVER, BLOCK)
    for s in range(2):
        far = jnp.where(core == 0, block(s, s + 4), block(s + 2, s + 6))
        out_ref[:, 16 + s] = far.reshape(SPLIT, SLIVER, BLOCK)


def inverse_factor(corr, inv_ref):
    panels = RANK // 8
    row = lax.broadcasted_iota(jnp.int32, (8, RANK), 0)
    lane = lax.broadcasted_iota(jnp.int32, (8, RANK), 1)
    left = [corr[8 * p : 8 * p + 8, :] for p in range(panels)]
    right = [jnp.where(lane == row + 8 * p, 1.0, 0.0) for p in range(panels)]
    least = jnp.full((1, RANK), jnp.inf, jnp.float32)
    for p in range(panels):
        here, there = left[p], right[p]
        column = [jnp.broadcast_to(here[:, 8 * p + k : 8 * p + k + 1], (8, RANK)) for k in range(8)]
        scale = jnp.zeros((8, RANK), jnp.float32)
        for k in range(8):
            pivot = column[k][k : k + 1, :]
            root = lax.rsqrt(pivot)
            least = jnp.minimum(least, pivot)
            factor = jnp.where(row > k, column[k] * root, 0.0)
            for later in range(k + 1, 8):
                column[later] = column[later] - factor * (column[later][k : k + 1, :] * root)
            here = here - factor * (here[k : k + 1, :] * root)
            there = there - factor * (there[k : k + 1, :] * root)
            scale = jnp.where(row == k, root, scale)
        here, there = here * scale, there * scale
        inv_ref[8 * p : 8 * p + 8, :] = there
        turned = here.T
        for q in range(p + 1, panels):
            part = turned[8 * q : 8 * q + 8, :]
            for k in range(8):
                factor = jnp.broadcast_to(part[:, k : k + 1], (8, RANK))
                left[q] = left[q] - factor * here[k : k + 1, :]
                right[q] = right[q] - factor * there[k : k + 1, :]
    return jnp.min(least)


def iterate_kernel(columns, place_ref, own_ref, twin_ref, initial_ref, field_ref, basis_ref, core_ref,
                   high_ref, low_ref, pair_ref, image_ref, inv_ref):
    core, mode = place_ref[0], place_ref[1]
    scale = 1.0 / columns

    def put(a, b, value):
        def at(index):
            return pl.ds(pl.multiple_of(index * BLOCK, BLOCK), BLOCK) if not isinstance(index, int) else pl.ds(index * BLOCK, BLOCK)

        value = value.reshape(BLOCK, BLOCK) * scale
        high, low = split_two(value)
        high_ref[at(a), at(b)] = high
        low_ref[at(a), at(b)] = low
        if not (isinstance(a, int) and a == b):
            high, low = split_two(value.T)
            high_ref[at(b), at(a)] = high
            low_ref[at(b), at(a)] = low

    for slot, (a, b) in enumerate(SLOTS):
        put(a, b, own_ref[:, slot])
        put((a + 4) % 8, (b + 4) % 8, twin_ref[:, slot])
    for s in range(2):
        put(2 * core + s, 2 * core + s + 4, own_ref[:, 16 + s])
        put(6 - 2 * core + s, 2 - 2 * core + s, twin_ref[:, 16 + s])

    def set_pair(rows, value):
        high, low = split_two(value)
        pair_ref[rows, :RANK] = high
        pair_ref[rows, RANK:] = low

    def start():
        for half in range(2):
            offset = pl.multiple_of(lax.rem(core * 512 + half * 512, ROWS), 512)
            set_pair(pl.ds(half * 512, 512), initial_ref[pl.ds(offset, 512), :RANK])

    def multiply():
        pair = pair_ref[...]
        total = jnp.zeros((1, RANK), jnp.float32)
        for r in range(4):
            rows = pl.ds(r * 256, 256)
            both = dot_nn(high_ref[rows, :], pair)
            small = dot_nn(low_ref[rows, :], pair[:, :RANK])
            image = both[:, :RANK] + (both[:, RANK:] + small)
            image_ref[rows, :] = image
            total = total + jnp.sum(image * image, axis=0, keepdims=True)
        root = lax.rsqrt(total)
        for r in range(4):
            rows = pl.ds(r * 256, 256)
            set_pair(rows, image_ref[rows, :] * root)

    def orthonormalise():
        pair = pair_ref[...]
        corr = dot_tn(pair, pair)
        corr = (corr[:RANK, :RANK] + corr[RANK:, RANK:]) + (corr[:RANK, RANK:] + corr[RANK:, :RANK])
        least = inverse_factor(corr, inv_ref)
        high, low = split_two(inv_ref[...])
        weights = jnp.concatenate(
            [jnp.concatenate([high, high], axis=1), jnp.concatenate([low, jnp.zeros_like(low)], axis=1)], axis=0
        )
        for r in range(4):
            rows = pl.ds(r * 256, 256)
            both = dot_nt(pair[r * 256 : (r + 1) * 256], weights)
            value = both[:, :RANK] + both[:, RANK:]
            image_ref[rows, :] = value
            set_pair(rows, value)
        return least

    def step(carry):
        i, stop = carry
        pl.when(jnp.logical_or(i == 0, i == ITERS))(start)
        multiply()
        least = lax.cond(i >= ITERS - 1, orthonormalise, lambda: jnp.float32(1.0))
        sound = least >= LEAST_PIVOT
        stop = jnp.where(jnp.logical_and(i == ITERS - 1, jnp.logical_not(sound)), 2 * ITERS, stop)
        return i + 1, stop

    lax.while_loop(lambda carry: carry[0] < carry[1], step, (jnp.int32(0), jnp.int32(ITERS)))

    own_rows = ROWS // SPLIT
    basis_ref[...] = image_ref[pl.ds(pl.multiple_of(lax.rem(mode * own_rows + core * 512, ROWS), own_rows), own_rows), :]
    total = jnp.zeros((RANK, field_ref.shape[1]), jnp.float32)
    for half in range(2):
        offset = pl.multiple_of(lax.rem(core * 512 + half * 512, ROWS), 512)
        total = total + dot_tn(pair_ref[pl.ds(half * 512, 512), :RANK], field_ref[pl.ds(offset, 512), :])
    core_ref[...] = total.reshape(core_ref.shape)


def on_device(unfolded, initial):
    cols = unfolded.shape[1] // SPLIT
    columns = unfolded.shape[1] * lax.axis_size("z") * lax.axis_size("core")
    core, mode = lax.axis_index("core"), lax.axis_index(MODE)
    place = jnp.stack([core, mode]).astype(jnp.int32)
    vmem = pl.BlockSpec(memory_space=pltpu.VMEM)
    smem = pl.BlockSpec(memory_space=pltpu.SMEM)

    wide = jnp.concatenate([initial, initial, initial], axis=1)
    whole_initial = lax.all_gather(wide, MODE, axis=0, tiled=True)

    own = lax.all_to_all(unfolded, MODE, split_axis=1, concat_axis=0, tiled=True)
    twin = lax.ppermute(own, "core", [(0, 1), (1, 0)])
    partial_gram = pl.pallas_call(
        gram_kernel,
        out_shape=jax.ShapeDtypeStruct((SPLIT, HALF_BLOCKS, SLIVER, BLOCK), jnp.float32),
        in_specs=[smem, vmem, vmem],
        out_specs=vmem,
        name="gram",
    )(place, own, twin)
    got = lax.all_to_all(partial_gram, MODE, split_axis=0, concat_axis=0, tiled=True)
    sliver = jnp.sum(got, axis=0)
    deep = lax.axis_size("z")
    sliver = jnp.pad(sliver, ((0, 2 * deep - HALF_BLOCKS), (0, 0), (0, 0))).reshape(deep, 2, SLIVER, BLOCK)
    got = lax.all_to_all(sliver, "z", split_axis=0, concat_axis=0, tiled=True)
    got = jnp.broadcast_to(jnp.sum(got, axis=0)[None], got.shape)
    got = lax.all_to_all(got, "z", split_axis=0, concat_axis=0, tiled=True)
    got = got.reshape(2 * deep, SLIVER, BLOCK)[:HALF_BLOCKS]
    got = jnp.broadcast_to(got[None], (SPLIT,) + got.shape)
    own_gram = lax.all_to_all(got, MODE, split_axis=0, concat_axis=0, tiled=True)
    twin_gram = lax.ppermute(own_gram, "core", [(0, 1), (1, 0)])

    basis, core_rows = pl.pallas_call(
        lambda *refs: iterate_kernel(columns, *refs),
        out_shape=(
            jax.ShapeDtypeStruct((ROWS // SPLIT, RANK), jnp.float32),
            jax.ShapeDtypeStruct((SPLIT, RANK // SPLIT, cols), jnp.float32),
        ),
        in_specs=[smem, vmem, vmem, vmem, vmem],
        out_specs=(vmem, vmem),
        scratch_shapes=[
            pltpu.VMEM((ROWS, ROWS), jnp.bfloat16),
            pltpu.VMEM((ROWS, ROWS), jnp.bfloat16),
            pltpu.VMEM((ROWS, 2 * RANK), jnp.bfloat16),
            pltpu.VMEM((ROWS, RANK), jnp.float32),
            pltpu.VMEM((RANK, RANK), jnp.float32),
        ],
        compiler_params=pltpu.CompilerParams(vmem_limit_bytes=40 * 1024 * 1024),
        name="iterate",
    )(place, own_gram, twin_gram, whole_initial, own)
    core_cols = lax.all_to_all(core_rows, MODE, split_axis=0, concat_axis=0, tiled=True)
    return basis, core_cols.transpose(1, 0, 2).reshape(RANK // SPLIT, SPLIT * cols)


def solution(mesh):
    chips = Mesh(mesh.devices.reshape(4, 4, mesh.devices.shape[1] // 2, 2), ("y", "x", "z", "core"))
    in_specs = (P(MODE, ("z", "core")), P(MODE, None))
    out_specs = (P(MODE, None), P(MODE, ("z", "core")))
    return jax.shard_map(on_device, mesh=chips, in_specs=in_specs, out_specs=out_specs, check_vma=False)
```

time: 964 us -> 203 us (0.21)
  waiting for transfers between devices: 742 us -> 21.6 us
  other arithmetic: 94.8 us -> 1.36 us
  Pallas kernels: 0 us -> 47.2 us
  starting transfers between devices: 0.65 us -> 27 us
  matrix products: 22.8 us -> 0 us
    psum x5 -> x0, waiting for transfers between devices: 647 us -> none  [the longest x4 459 us: on_device(): lax.psum(jnp.dot(image.T, image, precision=lax.Precision.HIGHEST), 'mode')]
    another operation x20 -> x1, other arithmetic: 91.4 us -> 0.64 us  [on_device(): place = jnp.stack([core, mode]).astype(jnp.int32)]
    all_gather x1, waiting for transfers between devices: 94.5 us -> 9.44 us  [on_device(): whole_initial = lax.all_gather(wide, MODE, axis=0, tiled=True)]
    all_to_all x1 -> x5, blocking collectives: 10.8 us -> 85 us  [the longest x1 22 us: on_device(): lax.all_to_all(partial_gram, MODE, split_axis=0, concat_axis=0, tiled=True)]
    all_gather x4 -> x0, blocking collectives: 71.7 us -> none  [on_device(): whole_basis = lax.all_gather(basis, 'mode', axis=0, tiled=True)]
    pallas_call x0 -> x2, Pallas kernels: none -> 47.2 us  [the longest x1 44.3 us: on_device(): pl.pallas_call(lambda *refs: iterate_kernel(columns, *refs), out_shape=(j...]
    dot_general x10 -> x0, matrix products: 21.4 us -> none  [the longest x1 6.93 us: on_device(): lax.dot_general(unfolded, slab, (((1,), (1,)), ((), ())), preferred_eleme...]
    all_to_all x0 -> x1, starting transfers between devices: none -> 14.9 us  [on_device(): got = lax.all_to_all(sliver, 'z', split_axis=0, concat_axis=0, tiled=True)]
  transfers between devices with their start and end apart: 6 -> 4, of which waited for: 6 -> 3; matrix products, arithmetic and copies ran while one was open for 0% -> 1% of each run, Pallas kernels for 0% -> 0%
where the time goes in v1:
time: 203 us; the launch traced here: 201 us
  blocking collectives  85 us (42%)
  Pallas kernels  47.2 us (23%)
  starting transfers between devices  27 us (13%)
  waiting for transfers between devices  21.6 us (11%)
  between operations  14.1 us (7%)
  local copies, waits for them, and re-layouts  4.74 us (2%)
    pallas_call x1, Pallas kernels, on_device(): pl.pallas_call(lambda *refs: iterate_kernel(columns, *refs), out_shape=(j...  44.3 us
    all_to_all x1, blocking collectives, on_device(): lax.all_to_all(partial_gram, MODE, split_axis=0, concat_axis=0, tiled=True)  22 us
    all_to_all x1, blocking collectives, on_device(): lax.all_to_all(got, MODE, split_axis=0, concat_axis=0, tiled=True)  17.6 us
    all_to_all x1, blocking collectives, on_device(): got = lax.all_to_all(got, 'z', split_axis=0, concat_axis=0, tiled=True)  17.2 us
    all_to_all x1, blocking collectives, on_device(): lax.all_to_all(unfolded, MODE, split_axis=1, concat_axis=0, tiled=True)  16.9 us
    all_to_all x1, starting transfers between devices, on_device(): got = lax.all_to_all(sliver, 'z', split_axis=0, concat_axis=0, tiled=True)  14.9 us
    all_to_all x1, blocking collectives, on_device(): lax.all_to_all(core_rows, MODE, split_axis=0, concat_axis=0, tiled=True)  11.3 us
    all_to_all x1, waiting for transfers between devices, on_device(): got = lax.all_to_all(sliver, 'z', split_axis=0, concat_axis=0, tiled=True)  11.2 us
  transfers between devices with their start and end apart: 4, of which 3 were waited for; matrix products, arithmetic and copies ran while one was open for 1% of the time, Pallas kernels for 0%

profile of v1, /device:TPU:1, one launch (start us, length us, event | category | flops | bytes accessed | tf_op | source)
XLA Modules:
  0.0 201.0 jit_solution(15492711878119618466)
XLA Ops:
  7.2 1.1 copy.8
  8.3 16.9 %all_to_all.44 = bf16[64,16,256]{2,0,1:T(8,128)(2,1)S(1)} all-to-all(bf16[64,16,256]{2,0,1:T(8,128)(2,1)S(1)} %bitcast.17), channel_id=1, replica_groups=mesh['y'=4,'x'=4,'z'=16,'core'=2] {'y','x'}, dimensions={1} | all-to-all | bytes 1048576 | tf_op jit(solution)/shard_map/all_to_all | solution.py:193
  25.2 0.0 copy-start
  25.2 4.9 %collective-permute-start = (bf16[1024,256]{1,0:T(8,128)(2,1)S(1)}, bf16[1024,256]{1,0:T(8,128)(2,1)S(1)}, u32[]{:S(2)}, u32[]{:S(2)}) collective-permute-start(bf16[1024,256]{1,0:T(8,128)(2,1)S(1)} %bitcast.14), channel_id=1, source_target_pairs={{0,1},{1,0},{2,3},{3,2},{4,5},{5,4},{6,7},{7,6},{8,9},{9,8},{10,11... | collective-permute-start | bytes 1572872 | tf_op jit(solution)/shard_map/ppermute | solution.py:194
  30.1 0.6 pad_add_fusion.place_ref.refs_0_
  30.7 0.9 collective-permute-done.twin_ref
  31.6 0.0 copy-done
  31.6 0.0 copy-start.4
  31.6 0.8 copy-done.4
  32.4 2.9 %gram.1 = f32[16,18,8,128]{3,2,1,0:T(8,128)} custom-call(s32[2]{0:T(128)} %pad_add_fusion.place_ref.refs_0_, bf16[1024,256]{1,0:T(8,128)(2,1)} %bitcast.15, bf16[1024,256]{1,0:T(8,128)(2,1)} %copy-done.4), custom_call_target="tpu_custom_call" | custom-call | tf_op jit(solution)/shard_map/gram/pallas_call | solution.py:195
  35.3 22.0 %all_to_all.45 = f32[16,18,8,128]{3,2,1,0:T(8,128)S(1)} all-to-all(f32[16,18,8,128]{3,2,1,0:T(8,128)} %gram.1), channel_id=1, replica_groups=mesh['y'=4,'x'=4,'z'=16,'core'=2] {'y','x'}, dimensions={0} | all-to-all | bytes 2359296 | tf_op jit(solution)/shard_map/all_to_all | solution.py:202
  57.3 0.0 copy-start.5
  57.3 0.1 reduce_sum.18
  57.3 0.7 pad.4
  58.0 14.9 %all-to-all-start.2 = ((f32[16,2,8,128]{3,2,1,0:T(8,128)}), f32[16,2,8,128]{3,2,1,0:T(8,128)S(1)}, u32[]{:S(2)}, u32[]{:S(2)}) async-start(f32[16,2,8,128]{3,2,1,0:T(8,128)} %bitcast.5), calls=%async_computation.2 | async-start | bytes 262144 | tf_op jit(solution)/shard_map/all_to_all | solution.py:206
  72.9 0.0 all-gather.2.cloned.1.call-start
  72.9 0.0 copy-done.5
  73.0 0.6 pad_maximum_fusion
  73.6 0.0 all-gather.2.cloned.1.call-update
  73.6 11.2 %all-to-all-done.2 = f32[16,2,8,128]{3,2,1,0:T(8,128)S(1)} async-done(((f32[16,2,8,128]{3,2,1,0:T(8,128)}), f32[16,2,8,128]{3,2,1,0:T(8,128)S(1)}, u32[]{:S(2)}, u32[]{:S(2)}) %all-to-all-start.2) | async-done | bytes 131104 | tf_op jit(solution)/shard_map/all_to_all | solution.py:206
  84.9 17.2 %all_to_all.46 = f32[16,2,8,128]{3,2,1,0:T(8,128)S(1)} all-to-all(f32[16,2,8,128]{3,2,1,0:T(8,128)S(1)} %broadcast_in_dim.6), channel_id=1, replica_groups=mesh['y'=4,'x'=4,'z'=16,'core'=2] {'z'}, dimensions={0} | all-to-all | bytes 262144 | tf_op jit(solution)/shard_map/all_to_all | solution.py:208
  102.1 0.1 broadcast_in_dim.16
  102.2 0.0 copy-start.1
  102.2 0.0 copy-start.3
  102.2 17.6 %all_to_all.47.refs_1_ = f32[16,18,8,128]{3,2,1,0:T(8,128)S(1)} all-to-all(f32[16,18,8,128]{3,2,1,0:T(8,128)S(1)} %broadcast_in_dim.16), channel_id=1, replica_groups=mesh['y'=4,'x'=4,'z'=16,'core'=2] {'y','x'}, dimensions={0} | all-to-all | bytes 2359296 | tf_op jit(solution)/shard_map/all_to_all | solution.py:211
  119.8 7.1 %collective-permute-start.1 = (f32[16,18,8,128]{3,2,1,0:T(8,128)S(1)}, f32[16,18,8,128]{3,2,1,0:T(8,128)S(1)}, u32[]{:S(2)}, u32[]{:S(2)}) collective-permute-start(f32[16,18,8,128]{3,2,1,0:T(8,128)S(1)} %all_to_all.47.refs_1_), channel_id=1, source_target_pairs={{0,1},{1,0},{2,3},{3,2},{4,5},{5,4},{6,7},{7,6},{8,9},{9,8},{10,11... | collective-permute-start | bytes 3538952 | tf_op jit(solution)/shard_map/ppermute | solution.py:212
  127.0 9.4 %all-gather.2.cloned.1.call-done.refs_3_ = f32[1024,384]{1,0:T(8,128)} async-done(((f32[64,384]{1,0:T(8,128)}), f32[1024,384]{1,0:T(8,128)}) %all-gather.2.cloned.1.call-update) | async-done | bytes 1572880 | tf_op jit(solution)/shard_map/all_gather | solution.py:191
  136.4 0.0 collective-permute-done.1.refs_2_
  136.4 0.0 copy-done.1
  136.4 0.0 copy-done.3
  136.4 0.0 copy-start.2
  136.4 1.4 copy-done.2
  137.8 44.3 %iterate.1 = (f32[64,128]{1,0:T(8,128)}, f32[16,8,256]{2,1,0:T(8,128)S(1)}) custom-call(s32[2]{0:T(128)S(1)} %copy-done.3, f32[16,18,8,128]{3,2,1,0:T(8,128)S(1)} %all_to_all.47.refs_1_, f32[16,18,8,128]{3,2,1,0:T(8,128)S(1)} %collective-permute-done.1.refs_2_, f32[1024,384]{1,0:T(8,128)S(1)} %copy-done.2, bf16[1024,256]{1,0:T(8,128)(2,1)S(1)} %bitcast.16), custom_call_target="tpu_custom_call" | custom-call | tf_op jit(solution)/shard_map/iterate/pallas_call | solution.py:214
  182.2 11.3 %all_to_all.48 = f32[16,8,256]{2,1,0:T(8,128)S(1)} all-to-all(f32[16,8,256]{2,1,0:T(8,128)S(1)} %get-tuple-element.5), channel_id=1, replica_groups=mesh['y'=4,'x'=4,'z'=16,'core'=2] {'y','x'}, dimensions={0} | all-to-all | bytes 262144 | tf_op jit(solution)/shard_map/all_to_all | solution.py:232
  193.5 0.7 copy.10
  (3 shorter events, 0.0 us)
Async XLA Ops:
  25.2 6.4 %copy-start = (bf16[64,16,256]{2,0,1:T(8,128)(2,1)}, bf16[64,16,256]{2,0,1:T(8,128)(2,1)S(1)}, u32[]{:S(2)}) copy-start(bf16[64,16,256]{2,0,1:T(8,128)(2,1)S(1)} %all_to_all.44) | copy-start | bytes 1572868
  25.2 6.4 %collective-permute-start = (bf16[1024,256]{1,0:T(8,128)(2,1)S(1)}, bf16[1024,256]{1,0:T(8,128)(2,1)S(1)}, u32[]{:S(2)}, u32[]{:S(2)}) collective-permute-start(bf16[1024,256]{1,0:T(8,128)(2,1)S(1)} %bitcast.14), channel_id=1, source_target_pairs={{0,1},{1,0},{2,3},{3,2},{4,5},{5,4},{6,7},{7,6},{8,9},{9,8},{10,11... | collective-permute-start | bytes 1572872 | tf_op jit(solution)/shard_map/ppermute | solution.py:194
  31.6 0.8 copy-start.4
  57.3 15.7 %copy-start.5 = (f32[64,128]{1,0:T(8,128)S(1)}, f32[64,128]{1,0:T(8,128)}, u32[]{:S(2)}) copy-start(f32[64,128]{1,0:T(8,128)} %param.3) | copy-start | bytes 98308
  58.0 26.9 %all-to-all-start.2 = ((f32[16,2,8,128]{3,2,1,0:T(8,128)}), f32[16,2,8,128]{3,2,1,0:T(8,128)S(1)}, u32[]{:S(2)}, u32[]{:S(2)}) async-start(f32[16,2,8,128]{3,2,1,0:T(8,128)} %bitcast.5), calls=%async_computation.2 | async-start | bytes 262144 | tf_op jit(solution)/shard_map/all_to_all | solution.py:206
  72.9 63.5 %all-gather.2.cloned.1.call-start = ((), (), s32[]{:S(2)}) async-start(), calls=%async_computation.6 | async-start | bytes 1671168 | tf_op jit(solution)/shard_map/all_gather | solution.py:191
  102.2 34.2 %copy-start.1 = (bf16[64,16,256]{2,0,1:T(8,128)(2,1)S(1)}, bf16[64,16,256]{2,0,1:T(8,128)(2,1)}, u32[]{:S(2)}) copy-start(bf16[64,16,256]{2,0,1:T(8,128)(2,1)} %copy-done) | copy-start | bytes 1572868
  102.2 34.2 %copy-start.3 = (s32[2]{0:T(128)S(1)}, s32[2]{0:T(128)}, u32[]{:S(2)}) copy-start(s32[2]{0:T(128)} %pad_add_fusion.place_ref.refs_0_) | copy-start | bytes 28
  119.8 16.6 %collective-permute-start.1 = (f32[16,18,8,128]{3,2,1,0:T(8,128)S(1)}, f32[16,18,8,128]{3,2,1,0:T(8,128)S(1)}, u32[]{:S(2)}, u32[]{:S(2)}) collective-permute-start(f32[16,18,8,128]{3,2,1,0:T(8,128)S(1)} %all_to_all.47.refs_1_), channel_id=1, source_target_pairs={{0,1},{1,0},{2,3},{3,2},{4,5},{5,4},{6,7},{7,6},{8,9},{9,8},{10,11... | collective-permute-start | bytes 3538952 | tf_op jit(solution)/shard_map/ppermute | solution.py:212
  136.4 1.4 copy-start.2
Sparse Core Ops, SparseCore 0:
  76.7 59.6 all-gather.1

commit v2 on v1

--- a/solution.py
+++ b/solution.py
@@ -37,10 +37,11 @@
 
 def gram_kernel(place_ref, own_ref, twin_ref, out_ref):
     core = place_ref[0]
+    cols = own_ref.shape[1] - RANK
 
     def rows(ref, a):
         start = pl.multiple_of(lax.rem(core * 512 + a * 256, ROWS), 256)
-        return ref[pl.ds(start, 256), :]
+        return ref[pl.ds(start, 256), :cols]
 
     own = [rows(own_ref, a) for a in range(4)]
     twin = [rows(twin_ref, a) for a in range(4)]
@@ -92,7 +93,7 @@
     return jnp.min(least)
 
 
-def iterate_kernel(columns, place_ref, own_ref, twin_ref, initial_ref, field_ref, basis_ref, core_ref,
+def iterate_kernel(columns, cols, place_ref, own_ref, twin_ref, field_ref, twin_field_ref, basis_ref, core_ref,
                    high_ref, low_ref, pair_ref, image_ref, inv_ref):
     core, mode = place_ref[0], place_ref[1]
     scale = 1.0 / columns
@@ -125,7 +126,10 @@
     def start():
         for half in range(2):
             offset = pl.multiple_of(lax.rem(core * 512 + half * 512, ROWS), 512)
-            set_pair(pl.ds(half * 512, 512), initial_ref[pl.ds(offset, 512), :RANK])
+            first = field_ref[pl.ds(offset, 512), cols:]
+            second = twin_field_ref[pl.ds(offset, 512), cols:]
+            pair_ref[pl.ds(half * 512, 512), :RANK] = jnp.where(core == 0, first, second)
+            pair_ref[pl.ds(half * 512, 512), RANK:] = jnp.where(core == 0, second, first)
 
     def multiply():
         pair = pair_ref[...]
@@ -172,49 +176,56 @@
 
     own_rows = ROWS // SPLIT
     basis_ref[...] = image_ref[pl.ds(pl.multiple_of(lax.rem(mode * own_rows + core * 512, ROWS), own_rows), own_rows), :]
-    total = jnp.zeros((RANK, field_ref.shape[1]), jnp.float32)
+    total = jnp.zeros((RANK, cols), jnp.float32)
     for half in range(2):
         offset = pl.multiple_of(lax.rem(core * 512 + half * 512, ROWS), 512)
-        total = total + dot_tn(pair_ref[pl.ds(half * 512, 512), :RANK], field_ref[pl.ds(offset, 512), :])
+        total = total + dot_tn(pair_ref[pl.ds(half * 512, 512), :RANK], field_ref[pl.ds(offset, 512), :cols])
     core_ref[...] = total.reshape(core_ref.shape)
 
 
 def on_device(unfolded, initial):
-    cols = unfolded.shape[1] // SPLIT
-    columns = unfolded.shape[1] * lax.axis_size("z") * lax.axis_size("core")
+    held, cols = unfolded.shape[0], unfolded.shape[1] // SPLIT
+    columns = unfolded.shape[1] * lax.axis_size("zh") * lax.axis_size("zl") * lax.axis_size("core")
     core, mode = lax.axis_index("core"), lax.axis_index(MODE)
     place = jnp.stack([core, mode]).astype(jnp.int32)
     vmem = pl.BlockSpec(memory_space=pltpu.VMEM)
     smem = pl.BlockSpec(memory_space=pltpu.SMEM)
-
-    wide = jnp.concatenate([initial, initial, initial], axis=1)
-    whole_initial = lax.all_gather(wide, MODE, axis=0, tiled=True)
-
-    own = lax.all_to_all(unfolded, MODE, split_axis=1, concat_axis=0, tiled=True)
-    twin = lax.ppermute(own, "core", [(0, 1), (1, 0)])
+    swap = [(0, 1), (1, 0)]
+
+    high = lax.reduce_precision(initial, exponent_bits=8, mantissa_bits=7)
+    half = jnp.where(core == 0, high, initial - high).astype(jnp.bfloat16)
+    parts = jnp.concatenate(
+        [
+            unfolded.reshape(held, SPLIT, cols).transpose(1, 0, 2),
+            jnp.broadcast_to(half[None], (SPLIT, held, RANK)),
+        ],
+        axis=2,
+    )
+    own = lax.all_to_all(parts, MODE, split_axis=0, concat_axis=0, tiled=True).reshape(ROWS, cols + RANK)
+    twin = lax.ppermute(own, "core", swap)
     partial_gram = pl.pallas_call(
         gram_kernel,
         out_shape=jax.ShapeDtypeStruct((SPLIT, HALF_BLOCKS, SLIVER, BLOCK), jnp.float32),
         in_specs=[smem, vmem, vmem],
         out_specs=vmem,
+        compiler_params=pltpu.CompilerParams(vmem_limit_bytes=16 * 1024 * 1024),
         name="gram",
     )(place, own, twin)
+
     got = lax.all_to_all(partial_gram, MODE, split_axis=0, concat_axis=0, tiled=True)
     sliver = jnp.sum(got, axis=0)
-    deep = lax.axis_size("z")
-    sliver = jnp.pad(sliver, ((0, 2 * deep - HALF_BLOCKS), (0, 0), (0, 0))).reshape(deep, 2, SLIVER, BLOCK)
-    got = lax.all_to_all(sliver, "z", split_axis=0, concat_axis=0, tiled=True)
-    got = jnp.broadcast_to(jnp.sum(got, axis=0)[None], got.shape)
-    got = lax.all_to_all(got, "z", split_axis=0, concat_axis=0, tiled=True)
-    got = got.reshape(2 * deep, SLIVER, BLOCK)[:HALF_BLOCKS]
-    got = jnp.broadcast_to(got[None], (SPLIT,) + got.shape)
+    got = jnp.broadcast_to(sliver[None], (lax.axis_size("zl"),) + sliver.shape)
+    got = lax.all_to_all(got, "zl", split_axis=0, concat_axis=0, tiled=True)
+    got = lax.all_gather(jnp.sum(got, axis=0), "zh", axis=0, tiled=False)
+    sliver = jnp.sum(got, axis=0)
+    got = jnp.broadcast_to(sliver[None], (SPLIT,) + sliver.shape)
     own_gram = lax.all_to_all(got, MODE, split_axis=0, concat_axis=0, tiled=True)
-    twin_gram = lax.ppermute(own_gram, "core", [(0, 1), (1, 0)])
+    twin_gram = lax.ppermute(own_gram, "core", swap)
 
     basis, core_rows = pl.pallas_call(
-        lambda *refs: iterate_kernel(columns, *refs),
+        lambda *refs: iterate_kernel(columns, cols, *refs),
         out_shape=(
-            jax.ShapeDtypeStruct((ROWS // SPLIT, RANK), jnp.float32),
+            jax.ShapeDtypeStruct((held, RANK), jnp.float32),
             jax.ShapeDtypeStruct((SPLIT, RANK // SPLIT, cols), jnp.float32),
         ),
         in_specs=[smem, vmem, vmem, vmem, vmem],
@@ -226,15 +237,16 @@
             pltpu.VMEM((ROWS, RANK), jnp.float32),
             pltpu.VMEM((RANK, RANK), jnp.float32),
         ],
-        compiler_params=pltpu.CompilerParams(vmem_limit_bytes=40 * 1024 * 1024),
+        compiler_params=pltpu.CompilerParams(vmem_limit_bytes=32 * 1024 * 1024),
         name="iterate",
-    )(place, own_gram, twin_gram, whole_initial, own)
+    )(place, own_gram, twin_gram, own, twin)
     core_cols = lax.all_to_all(core_rows, MODE, split_axis=0, concat_axis=0, tiled=True)
     return basis, core_cols.transpose(1, 0, 2).reshape(RANK // SPLIT, SPLIT * cols)
 
 
 def solution(mesh):
-    chips = Mesh(mesh.devices.reshape(4, 4, mesh.devices.shape[1] // 2, 2), ("y", "x", "z", "core"))
-    in_specs = (P(MODE, ("z", "core")), P(MODE, None))
-    out_specs = (P(MODE, None), P(MODE, ("z", "core")))
+    chips = Mesh(mesh.devices.reshape(4, 4, 4, mesh.devices.shape[1] // 8, 2), ("y", "x", "zh", "zl", "core"))
+    rest = ("zh", "zl", "core")
+    in_specs = (P(MODE, rest), P(MODE, None))
+    out_specs = (P(MODE, None), P(MODE, rest))
     return jax.shard_map(on_device, mesh=chips, in_specs=in_specs, out_specs=out_specs, check_vma=False)

time: 203 us -> 170 us (0.84)
  blocking collectives: 85 us -> 103 us
  waiting for transfers between devices: 21.6 us -> 4.26 us
  starting transfers between devices: 27 us -> 13.3 us
  between operations: 14.1 us -> 0.72 us
  local copies, waits for them, and re-layouts: 4.74 us -> 1.88 us
    all_gather x0 -> x1, blocking collectives: none -> 25.8 us  [on_device(): got = lax.all_gather(jnp.sum(got, axis=0), 'zh', axis=0, tiled=False)]
    all_to_all x1 -> x0, starting transfers between devices: 14.9 us -> none  [on_device(): got = lax.all_to_all(sliver, 'z', split_axis=0, concat_axis=0, tiled=True)]
    all_to_all x1 -> x0, waiting for transfers between devices: 11.2 us -> none  [on_device(): got = lax.all_to_all(sliver, 'z', split_axis=0, concat_axis=0, tiled=True)]
    all_gather x1 -> x0, waiting for transfers between devices: 9.44 us -> none  [on_device(): whole_initial = lax.all_gather(wide, MODE, axis=0, tiled=True)]
    ppermute x2, waiting for transfers between devices: 0.87 us -> 4.26 us  [the longest x1 2.45 us: on_device(): twin_gram = lax.ppermute(own_gram, 'core', swap)]
    all_to_all x2, blocking collectives: 34.1 us -> 31.3 us  [the longest x1 19.6 us: on_device(): lax.all_to_all(parts, MODE, split_axis=0, concat_axis=0, tiled=True)]
    unnamed x13 -> x1, local copies, waits for them, and re-layouts: 2.9 us -> 0.66 us
  transfers between devices with their start and end apart: 4 -> 2, of which waited for: 3 -> 2; matrix products, arithmetic and copies ran while one was open for 1% -> 0% of each run, Pallas kernels for 0% -> 0%
where the time goes in v2:
time: 170 us
  blocking collectives  103 us (61%)
  Pallas kernels  45.5 us (27%)
  starting transfers between devices  13.3 us (8%)
  waiting for transfers between devices  4.26 us (3%)
  local copies, waits for them, and re-layouts  1.88 us (1%)
    pallas_call x1, Pallas kernels, on_device(): pl.pallas_call(lambda *refs: iterate_kernel(columns, cols, *refs), out_sh...  44.3 us
    all_gather x1, blocking collectives, on_device(): got = lax.all_gather(jnp.sum(got, axis=0), 'zh', axis=0, tiled=False)  25.8 us
    all_to_all x1, blocking collectives, on_device(): lax.all_to_all(partial_gram, MODE, split_axis=0, concat_axis=0, tiled=True)  20.6 us
    all_to_all x1, blocking collectives, on_device(): lax.all_to_all(parts, MODE, split_axis=0, concat_axis=0, tiled=True)  19.6 us
    all_to_all x1, blocking collectives, on_device(): lax.all_to_all(got, MODE, split_axis=0, concat_axis=0, tiled=True)  15.8 us
    all_to_all x1, blocking collectives, on_device(): got = lax.all_to_all(got, 'zl', split_axis=0, concat_axis=0, tiled=True)  11.7 us
    all_to_all x1, blocking collectives, on_device(): lax.all_to_all(core_rows, MODE, split_axis=0, concat_axis=0, tiled=True)  9.63 us
    ppermute x1, starting transfers between devices, on_device(): twin_gram = lax.ppermute(own_gram, 'core', swap)  8.24 us
  transfers between devices with their start and end apart: 2, of which 2 were waited for; matrix products, arithmetic and copies ran while one was open for 0% of the time, Pallas kernels for 0%

profile of v2, /device:TPU:1, one launch (start us, length us, event | category | flops | bytes accessed | tf_op | source)
XLA Modules:
  0.0 169.9 jit_solution(11986214744450527407)
XLA Ops:
  0.6 1.1 copy.9
  1.7 0.8 fusion
  2.6 0.1 pad_maximum_fusion
  2.6 19.6 %all_to_all.25 = bf16[16,64,384]{2,1,0:T(8,128)(2,1)S(1)} all-to-all(bf16[16,64,384]{2,1,0:T(8,128)(2,1)S(1)} %pad_maximum_fusion), channel_id=1, replica_groups=mesh['y'=4,'x'=4,'zh'=4,'zl'=4,'core'=2] {'y','x'}, dimensions={0} | all-to-all | bytes 1572864 | tf_op jit(solution)/shard_map/all_to_all | solution.py:204
  22.3 5.0 %collective-permute-start = (bf16[1024,384]{1,0:T(8,128)(2,1)S(1)}, bf16[1024,384]{1,0:T(8,128)(2,1)S(1)}, u32[]{:S(2)}, u32[]{:S(2)}) collective-permute-start(bf16[1024,384]{1,0:T(8,128)(2,1)S(1)} %bitcast.14), channel_id=1, source_target_pairs={{0,1},{1,0},{2,3},{3,2},{4,5},{5,4},{6,7},{7,6},{8,9},{9,8},{10,11... | collective-permute-start | bytes 2359304 | tf_op jit(solution)/shard_map/ppermute | solution.py:205
  27.3 0.1 pad_add_fusion.place_ref.refs_0_
  27.4 1.8 %collective-permute-done.twin_ref.refs_4_ = bf16[1024,384]{1,0:T(8,128)(2,1)S(1)} collective-permute-done((bf16[1024,384]{1,0:T(8,128)(2,1)S(1)}, bf16[1024,384]{1,0:T(8,128)(2,1)S(1)}, u32[]{:S(2)}, u32[]{:S(2)}) %collective-permute-start) | collective-permute-done | bytes 786464 | tf_op jit(solution)/shard_map/ppermute | solution.py:205
  29.2 1.2 gram.1
  30.3 20.6 %all_to_all.26 = f32[16,18,8,128]{3,2,1,0:T(8,128)S(1)} all-to-all(f32[16,18,8,128]{3,2,1,0:T(8,128)S(1)} %gram.1), channel_id=1, replica_groups=mesh['y'=4,'x'=4,'zh'=4,'zl'=4,'core'=2] {'y','x'}, dimensions={0} | all-to-all | bytes 2359296 | tf_op jit(solution)/shard_map/all_to_all | solution.py:215
  51.0 0.1 reduce_sum.27
  51.1 11.7 %all_to_all.27 = f32[4,18,8,128]{3,2,1,0:T(8,128)S(1)} all-to-all(f32[4,18,8,128]{3,2,1,0:T(8,128)S(1)} %broadcast_in_dim.7), channel_id=1, replica_groups=mesh['y'=4,'x'=4,'zh'=4,'zl'=4,'core'=2] {'zl'}, dimensions={0} | all-to-all | bytes 589824 | tf_op jit(solution)/shard_map/all_to_all | solution.py:218
  62.8 25.8 %all-gather = f32[72,8,128]{2,1,0:T(8,128)S(1)} all-gather(f32[18,8,128]{2,1,0:T(8,128)S(1)} %reduce_sum.28), channel_id=2, replica_groups=mesh['y'=4,'x'=4,'zh'=4,'zl'=4,'core'=2] {'zh'}, dimensions={0}, use_global_device_ids=true | all-gather | bytes 368640 | tf_op jit(solution)/shard_map/all_gather | solution.py:219
  88.6 0.1 broadcast_in_dim.8
  88.7 15.8 %all_to_all.28.refs_1_ = f32[16,18,8,128]{3,2,1,0:T(8,128)S(1)} all-to-all(f32[16,18,8,128]{3,2,1,0:T(8,128)S(1)} %broadcast_in_dim.8), channel_id=1, replica_groups=mesh['y'=4,'x'=4,'zh'=4,'zl'=4,'core'=2] {'y','x'}, dimensions={0} | all-to-all | bytes 2359296 | tf_op jit(solution)/shard_map/all_to_all | solution.py:222
  104.5 8.2 %collective-permute-start.1 = (f32[16,18,8,128]{3,2,1,0:T(8,128)S(1)}, f32[16,18,8,128]{3,2,1,0:T(8,128)S(1)}, u32[]{:S(2)}, u32[]{:S(2)}) collective-permute-start(f32[16,18,8,128]{3,2,1,0:T(8,128)S(1)} %all_to_all.28.refs_1_), channel_id=1, source_target_pairs={{0,1},{1,0},{2,3},{3,2},{4,5},{5,4},{6,7},{7,6},{8,9},{9,8},{10,11... | collective-permute-start | bytes 3538952 | tf_op jit(solution)/shard_map/ppermute | solution.py:223
  112.8 2.5 %collective-permute-done.1.refs_2_ = f32[16,18,8,128]{3,2,1,0:T(8,128)S(1)} collective-permute-done((f32[16,18,8,128]{3,2,1,0:T(8,128)S(1)}, f32[16,18,8,128]{3,2,1,0:T(8,128)S(1)}, u32[]{:S(2)}, u32[]{:S(2)}) %collective-permute-start.1) | collective-permute-done | bytes 1179680 | tf_op jit(solution)/shard_map/ppermute | solution.py:223
  115.2 44.3 %iterate.1 = (f32[64,128]{1,0:T(8,128)}, f32[16,8,256]{2,1,0:T(8,128)S(1)}) custom-call(s32[2]{0:T(128)S(1)} %pad_add_fusion.place_ref.refs_0_, f32[16,18,8,128]{3,2,1,0:T(8,128)S(1)} %all_to_all.28.refs_1_, f32[16,18,8,128]{3,2,1,0:T(8,128)S(1)} %collective-permute-done.1.refs_2_, bf16[1024,384]{1,0:T(8,128)(2,1)S(1)} %bitcast.16, ...), custom_call_target="tpu_custom_call" | custom-call | tf_op jit(solution)/shard_map/iterate/pallas_call | solution.py:225
  159.6 9.6 %all_to_all.29 = f32[16,8,256]{2,1,0:T(8,128)S(1)} all-to-all(f32[16,8,256]{2,1,0:T(8,128)S(1)} %get-tuple-element.5), channel_id=1, replica_groups=mesh['y'=4,'x'=4,'zh'=4,'zl'=4,'core'=2] {'y','x'}, dimensions={0} | all-to-all | bytes 262144 | tf_op jit(solution)/shard_map/all_to_all | solution.py:243
  169.2 0.7 copy.11
  (4 shorter events, 0.1 us)
Async XLA Ops:
  22.3 6.9 %collective-permute-start = (bf16[1024,384]{1,0:T(8,128)(2,1)S(1)}, bf16[1024,384]{1,0:T(8,128)(2,1)S(1)}, u32[]{:S(2)}, u32[]{:S(2)}) collective-permute-start(bf16[1024,384]{1,0:T(8,128)(2,1)S(1)} %bitcast.14), channel_id=1, source_target_pairs={{0,1},{1,0},{2,3},{3,2},{4,5},{5,4},{6,7},{7,6},{8,9},{9,8},{10,11... | collective-permute-start | bytes 2359304 | tf_op jit(solution)/shard_map/ppermute | solution.py:205
  104.5 10.7 %collective-permute-start.1 = (f32[16,18,8,128]{3,2,1,0:T(8,128)S(1)}, f32[16,18,8,128]{3,2,1,0:T(8,128)S(1)}, u32[]{:S(2)}, u32[]{:S(2)}) collective-permute-start(f32[16,18,8,128]{3,2,1,0:T(8,128)S(1)} %all_to_all.28.refs_1_), channel_id=1, source_target_pairs={{0,1},{1,0},{2,3},{3,2},{4,5},{5,4},{6,7},{7,6},{8,9},{9,8},{10,11... | collective-permute-start | bytes 3538952 | tf_op jit(solution)/shard_map/ppermute | solution.py:223

commit v3 on v2

--- a/solution.py
+++ b/solution.py
@@ -13,6 +13,7 @@
 SPLIT = 16
 SLIVER = BLOCK // SPLIT
 LEAST_PIVOT = 2e-3
+CHUNK = 256
 MODE = ("y", "x")
 
 SLOTS = [(t, t + d) for t in range(4) for d in range(4)]
@@ -66,43 +67,63 @@
     lane = lax.broadcasted_iota(jnp.int32, (8, RANK), 1)
     left = [corr[8 * p : 8 * p + 8, :] for p in range(panels)]
     right = [jnp.where(lane == row + 8 * p, 1.0, 0.0) for p in range(panels)]
-    least = jnp.full((1, RANK), jnp.inf, jnp.float32)
+    least = jnp.full((8, RANK), jnp.inf, jnp.float32)
+
+    def columns_of(value, p):
+        return [jnp.broadcast_to(value[:, 8 * p + k : 8 * p + k + 1], (8, RANK)) for k in range(8)]
+
     for p in range(panels):
         here, there = left[p], right[p]
-        column = [jnp.broadcast_to(here[:, 8 * p + k : 8 * p + k + 1], (8, RANK)) for k in range(8)]
-        scale = jnp.zeros((8, RANK), jnp.float32)
-        for k in range(8):
-            pivot = column[k][k : k + 1, :]
-            root = lax.rsqrt(pivot)
-            least = jnp.minimum(least, pivot)
-            factor = jnp.where(row > k, column[k] * root, 0.0)
-            for later in range(k + 1, 8):
-                column[later] = column[later] - factor * (column[later][k : k + 1, :] * root)
-            here = here - factor * (here[k : k + 1, :] * root)
-            there = there - factor * (there[k : k + 1, :] * root)
-            scale = jnp.where(row == k, root, scale)
-        here, there = here * scale, there * scale
-        inv_ref[8 * p : 8 * p + 8, :] = there
-        turned = here.T
+        column = columns_of(here, p)
+        pivots = jnp.zeros((8, RANK), jnp.float32)
+        steps = []
+        for k in range(0, 8, 2):
+            first, second = column[k], column[k + 1]
+            a, b, c = first[k : k + 1], first[k + 1 : k + 2], second[k + 1 : k + 2]
+            det = a * c - b * b
+            inv_a, inv_det = 1.0 / a, 1.0 / det
+            ratio, inv_c = b * inv_a, a * inv_det
+            pivots = jnp.where(row == k, a, jnp.where(row == k + 1, det * inv_a, pivots))
+            lower = jnp.where(row > k, first, 0.0)
+            lowest = jnp.where(row > k + 1, second - first * ratio, 0.0)
+
+            def heads(value):
+                one = value[k : k + 1]
+                two = (value[k + 1 : k + 2] - ratio * one) * inv_c
+                return one * inv_a, two
+
+            tops = [heads(column[later]) for later in range(k + 2, 8)]
+            for later, (one, two) in zip(range(k + 2, 8), tops):
+                column[later] = column[later] - lower * one - lowest * two
+            sides = heads(here), heads(there)
+            here = here - lower * sides[0][0] - lowest * sides[0][1]
+            there = there - lower * sides[1][0] - lowest * sides[1][1]
+            steps.append((k, ratio, tops, sides))
+        least = jnp.minimum(least, pivots)
+        inv_ref[8 * p : 8 * p + 8, :] = there * lax.rsqrt(pivots)
         for q in range(p + 1, panels):
-            part = turned[8 * q : 8 * q + 8, :]
-            for k in range(8):
-                factor = jnp.broadcast_to(part[:, k : k + 1], (8, RANK))
-                left[q] = left[q] - factor * here[k : k + 1, :]
-                right[q] = right[q] - factor * there[k : k + 1, :]
+            column = columns_of(left[q], p)
+            for k, ratio, tops, sides in steps:
+                lower = column[k]
+                lowest = column[k + 1] - lower * ratio
+                for later, (one, two) in zip(range(k + 2, 8), tops):
+                    column[later] = column[later] - lower * one - lowest * two
+                left[q] = left[q] - lower * sides[0][0] - lowest * sides[0][1]
+                right[q] = right[q] - lower * sides[1][0] - lowest * sides[1][1]
     return jnp.min(least)
 
 
-def iterate_kernel(columns, cols, place_ref, own_ref, twin_ref, field_ref, twin_field_ref, basis_ref, core_ref,
+def iterate_kernel(cols, place_ref, own_ref, twin_ref, field_ref, twin_field_ref, basis_ref, core_ref,
                    high_ref, low_ref, pair_ref, image_ref, inv_ref):
     core, mode = place_ref[0], place_ref[1]
-    scale = 1.0 / columns
+    row = lax.broadcasted_iota(jnp.int32, (RANK, RANK), 0)
+    diagonal = row == lax.broadcasted_iota(jnp.int32, (RANK, RANK), 1)
+    largest = jnp.zeros((BLOCK, BLOCK), jnp.float32)
+
+    def at(index):
+        return pl.ds(index * BLOCK if isinstance(index, int) else pl.multiple_of(index * BLOCK, BLOCK), BLOCK)
 
     def put(a, b, value):
-        def at(index):
-            return pl.ds(pl.multiple_of(index * BLOCK, BLOCK), BLOCK) if not isinstance(index, int) else pl.ds(index * BLOCK, BLOCK)
-
-        value = value.reshape(BLOCK, BLOCK) * scale
         high, low = split_two(value)
         high_ref[at(a), at(b)] = high
         low_ref[at(a), at(b)] = low
@@ -112,80 +133,87 @@
             low_ref[at(b), at(a)] = low
 
     for slot, (a, b) in enumerate(SLOTS):
-        put(a, b, own_ref[:, slot])
-        put((a + 4) % 8, (b + 4) % 8, twin_ref[:, slot])
+        for ref, shift in ((own_ref, 0), (twin_ref, 4)):
+            value = ref[:, slot].reshape(BLOCK, BLOCK)
+            if a == b:
+                largest = jnp.maximum(largest, jnp.where(diagonal, value, 0.0))
+            put((a + shift) % 8, (b + shift) % 8, value)
     for s in range(2):
-        put(2 * core + s, 2 * core + s + 4, own_ref[:, 16 + s])
-        put(6 - 2 * core + s, 2 - 2 * core + s, twin_ref[:, 16 + s])
-
-    def set_pair(rows, value):
+        put(2 * core + s, 2 * core + s + 4, own_ref[:, 16 + s].reshape(BLOCK, BLOCK))
+        put(6 - 2 * core + s, 2 - 2 * core + s, twin_ref[:, 16 + s].reshape(BLOCK, BLOCK))
+    scale = 1.0 / jnp.max(largest)
+
+    def set_pair(side, rows, value):
         high, low = split_two(value)
-        pair_ref[rows, :RANK] = high
-        pair_ref[rows, RANK:] = low
+        pair_ref[side, rows, :RANK] = high
+        pair_ref[side, rows, RANK:] = low
 
     def start():
         for half in range(2):
             offset = pl.multiple_of(lax.rem(core * 512 + half * 512, ROWS), 512)
+            rows = pl.ds(half * 512, 512)
             first = field_ref[pl.ds(offset, 512), cols:]
             second = twin_field_ref[pl.ds(offset, 512), cols:]
-            pair_ref[pl.ds(half * 512, 512), :RANK] = jnp.where(core == 0, first, second)
-            pair_ref[pl.ds(half * 512, 512), RANK:] = jnp.where(core == 0, second, first)
-
-    def multiply():
-        pair = pair_ref[...]
-        total = jnp.zeros((1, RANK), jnp.float32)
-        for r in range(4):
-            rows = pl.ds(r * 256, 256)
-            both = dot_nn(high_ref[rows, :], pair)
-            small = dot_nn(low_ref[rows, :], pair[:, :RANK])
-            image = both[:, :RANK] + (both[:, RANK:] + small)
-            image_ref[rows, :] = image
-            total = total + jnp.sum(image * image, axis=0, keepdims=True)
-        root = lax.rsqrt(total)
-        for r in range(4):
-            rows = pl.ds(r * 256, 256)
-            set_pair(rows, image_ref[rows, :] * root)
-
-    def orthonormalise():
-        pair = pair_ref[...]
-        corr = dot_tn(pair, pair)
+            pair_ref[0, rows, :RANK] = jnp.where(core == 0, first, second)
+            pair_ref[0, rows, RANK:] = jnp.where(core == 0, second, first)
+
+    def multiply(side):
+        for r in range(ROWS // CHUNK):
+            rows = pl.ds(r * CHUNK, CHUNK)
+            both = dot_nn(high_ref[rows, :], pair_ref[side])
+            small = dot_nn(low_ref[rows, :], pair_ref[side, :, :RANK])
+            set_pair(1 - side, rows, (both[:, :RANK] + (both[:, RANK:] + small)) * scale)
+
+    def orthonormalise(side):
+        corr = dot_tn(pair_ref[side], pair_ref[side])
         corr = (corr[:RANK, :RANK] + corr[RANK:, RANK:]) + (corr[:RANK, RANK:] + corr[RANK:, :RANK])
-        least = inverse_factor(corr, inv_ref)
-        high, low = split_two(inv_ref[...])
+        squares = jnp.where(diagonal, corr, 0.0)
+        across = lax.rsqrt(jnp.sum(squares, axis=0, keepdims=True))
+        down = lax.rsqrt(jnp.sum(squares, axis=1, keepdims=True))
+        least = inverse_factor(corr * across * down, inv_ref)
+        high, low = split_two(inv_ref[...] * across)
         weights = jnp.concatenate(
             [jnp.concatenate([high, high], axis=1), jnp.concatenate([low, jnp.zeros_like(low)], axis=1)], axis=0
         )
         for r in range(4):
             rows = pl.ds(r * 256, 256)
-            both = dot_nt(pair[r * 256 : (r + 1) * 256], weights)
+            both = dot_nt(pair_ref[side, rows, :], weights)
             value = both[:, :RANK] + both[:, RANK:]
             image_ref[rows, :] = value
-            set_pair(rows, value)
+            set_pair(0, rows, value)
         return least
 
     def step(carry):
         i, stop = carry
-        pl.when(jnp.logical_or(i == 0, i == ITERS))(start)
-        multiply()
-        least = lax.cond(i >= ITERS - 1, orthonormalise, lambda: jnp.float32(1.0))
+
+        @pl.when(i == 0)
+        def _():
+            start()
+            for n in range(ITERS):
+                multiply(n % 2)
+
+        @pl.when(i > 0)
+        def _():
+            pl.when(i == 1)(start)
+            multiply(0)
+
+        least = orthonormalise(jnp.where(i == 0, ITERS % 2, 1))
         sound = least >= LEAST_PIVOT
-        stop = jnp.where(jnp.logical_and(i == ITERS - 1, jnp.logical_not(sound)), 2 * ITERS, stop)
-        return i + 1, stop
-
-    lax.while_loop(lambda carry: carry[0] < carry[1], step, (jnp.int32(0), jnp.int32(ITERS)))
+        return i + 1, jnp.where(jnp.logical_and(i == 0, jnp.logical_not(sound)), ITERS + 1, stop)
+
+    lax.while_loop(lambda carry: carry[0] < carry[1], step, (jnp.int32(0), jnp.int32(1)))
 
     own_rows = ROWS // SPLIT
     basis_ref[...] = image_ref[pl.ds(pl.multiple_of(lax.rem(mode * own_rows + core * 512, ROWS), own_rows), own_rows), :]
     total = jnp.zeros((RANK, cols), jnp.float32)
     for half in range(2):
         offset = pl.multiple_of(lax.rem(core * 512 + half * 512, ROWS), 512)
-        total = total + dot_tn(pair_ref[pl.ds(half * 512, 512), :RANK], field_ref[pl.ds(offset, 512), :cols])
+        total = total + dot_tn(pair_ref[0, pl.ds(half * 512, 512), :RANK], field_ref[pl.ds(offset, 512), :cols])
     core_ref[...] = total.reshape(core_ref.shape)
 
 
 def on_device(unfolded, initial):
     held, cols = unfolded.shape[0], unfolded.shape[1] // SPLIT
-    columns = unfolded.shape[1] * lax.axis_size("zh") * lax.axis_size("zl") * lax.axis_size("core")
     core, mode = lax.axis_index("core"), lax.axis_index(MODE)
     place = jnp.stack([core, mode]).astype(jnp.int32)
     vmem = pl.BlockSpec(memory_space=pltpu.VMEM)
@@ -223,7 +251,7 @@
     twin_gram = lax.ppermute(own_gram, "core", swap)
 
     basis, core_rows = pl.pallas_call(
-        lambda *refs: iterate_kernel(columns, cols, *refs),
+        lambda *refs: iterate_kernel(cols, *refs),
         out_shape=(
             jax.ShapeDtypeStruct((held, RANK), jnp.float32),
             jax.ShapeDtypeStruct((SPLIT, RANK // SPLIT, cols), jnp.float32),
@@ -233,7 +261,7 @@
         scratch_shapes=[
             pltpu.VMEM((ROWS, ROWS), jnp.bfloat16),
             pltpu.VMEM((ROWS, ROWS), jnp.bfloat16),
-            pltpu.VMEM((ROWS, 2 * RANK), jnp.bfloat16),
+            pltpu.VMEM((2, ROWS, 2 * RANK), jnp.bfloat16),
             pltpu.VMEM((ROWS, RANK), jnp.float32),
             pltpu.VMEM((RANK, RANK), jnp.float32),
         ],

time: 170 us -> 158 us (0.929)
  Pallas kernels: 45.5 us -> 32.8 us
    pallas_call x1, Pallas kernels: 44.3 us -> 31.6 us  [on_device(): pl.pallas_call(lambda *refs: iterate_kernel(cols, *refs), out_shape=(jax....]
where the time goes in v3:
time: 158 us; the launch traced here: 157 us
  blocking collectives  103 us (65%)
  Pallas kernels  32.8 us (21%)
  starting transfers between devices  13.5 us (9%)
  waiting for transfers between devices  4.08 us (3%)
  local copies, waits for them, and re-layouts  1.88 us (1%)
    pallas_call x1, Pallas kernels, on_device(): pl.pallas_call(lambda *refs: iterate_kernel(cols, *refs), out_shape=(jax....  31.6 us
    all_gather x1, blocking collectives, on_device(): got = lax.all_gather(jnp.sum(got, axis=0), 'zh', axis=0, tiled=False)  24.6 us
    all_to_all x1, blocking collectives, on_device(): lax.all_to_all(partial_gram, MODE, split_axis=0, concat_axis=0, tiled=True)  20.7 us
    all_to_all x1, blocking collectives, on_device(): lax.all_to_all(parts, MODE, split_axis=0, concat_axis=0, tiled=True)  19.6 us
    all_to_all x1, blocking collectives, on_device(): lax.all_to_all(got, MODE, split_axis=0, concat_axis=0, tiled=True)  15.8 us
    all_to_all x1, blocking collectives, on_device(): got = lax.all_to_all(got, 'zl', split_axis=0, concat_axis=0, tiled=True)  12.8 us
    all_to_all x1, blocking collectives, on_device(): lax.all_to_all(core_rows, MODE, split_axis=0, concat_axis=0, tiled=True)  9.63 us
    ppermute x1, starting transfers between devices, on_device(): twin_gram = lax.ppermute(own_gram, 'core', swap)  8.49 us
  transfers between devices with their start and end apart: 2, of which 2 were waited for; matrix products, arithmetic and copies ran while one was open for 0% of the time, Pallas kernels for 0%

profile of v3, /device:TPU:1, one launch (start us, length us, event | category | flops | bytes accessed | tf_op | source)
XLA Modules:
  0.0 157.1 jit_solution(1717457146341819580)
XLA Ops:
  0.6 1.1 copy.9
  1.7 0.8 fusion
  2.6 0.1 pad_maximum_fusion
  2.6 19.6 %all_to_all.25 = bf16[16,64,384]{2,1,0:T(8,128)(2,1)S(1)} all-to-all(bf16[16,64,384]{2,1,0:T(8,128)(2,1)S(1)} %pad_maximum_fusion), channel_id=1, replica_groups=mesh['y'=4,'x'=4,'zh'=4,'zl'=4,'core'=2] {'y','x'}, dimensions={0} | all-to-all | bytes 1572864 | tf_op jit(solution)/shard_map/all_to_all | solution.py:232
  22.3 5.0 %collective-permute-start = (bf16[1024,384]{1,0:T(8,128)(2,1)S(1)}, bf16[1024,384]{1,0:T(8,128)(2,1)S(1)}, u32[]{:S(2)}, u32[]{:S(2)}) collective-permute-start(bf16[1024,384]{1,0:T(8,128)(2,1)S(1)} %bitcast.14), channel_id=1, source_target_pairs={{0,1},{1,0},{2,3},{3,2},{4,5},{5,4},{6,7},{7,6},{8,9},{9,8},{10,11... | collective-permute-start | bytes 2359304 | tf_op jit(solution)/shard_map/ppermute | solution.py:233
  27.3 0.1 pad_add_fusion.place_ref.refs_0_
  27.4 1.8 %collective-permute-done.twin_ref.refs_4_ = bf16[1024,384]{1,0:T(8,128)(2,1)S(1)} collective-permute-done((bf16[1024,384]{1,0:T(8,128)(2,1)S(1)}, bf16[1024,384]{1,0:T(8,128)(2,1)S(1)}, u32[]{:S(2)}, u32[]{:S(2)}) %collective-permute-start) | collective-permute-done | bytes 786464 | tf_op jit(solution)/shard_map/ppermute | solution.py:233
  29.2 1.2 gram.1
  30.3 20.7 %all_to_all.26 = f32[16,18,8,128]{3,2,1,0:T(8,128)S(1)} all-to-all(f32[16,18,8,128]{3,2,1,0:T(8,128)S(1)} %gram.1), channel_id=1, replica_groups=mesh['y'=4,'x'=4,'zh'=4,'zl'=4,'core'=2] {'y','x'}, dimensions={0} | all-to-all | bytes 2359296 | tf_op jit(solution)/shard_map/all_to_all | solution.py:243
  51.0 0.1 reduce_sum.27
  51.1 12.8 %all_to_all.27 = f32[4,18,8,128]{3,2,1,0:T(8,128)S(1)} all-to-all(f32[4,18,8,128]{3,2,1,0:T(8,128)S(1)} %broadcast_in_dim.7), channel_id=1, replica_groups=mesh['y'=4,'x'=4,'zh'=4,'zl'=4,'core'=2] {'zl'}, dimensions={0} | all-to-all | bytes 589824 | tf_op jit(solution)/shard_map/all_to_all | solution.py:246
  63.9 24.6 %all-gather = f32[72,8,128]{2,1,0:T(8,128)S(1)} all-gather(f32[18,8,128]{2,1,0:T(8,128)S(1)} %reduce_sum.28), channel_id=2, replica_groups=mesh['y'=4,'x'=4,'zh'=4,'zl'=4,'core'=2] {'zh'}, dimensions={0}, use_global_device_ids=true | all-gather | bytes 368640 | tf_op jit(solution)/shard_map/all_gather | solution.py:247
  88.5 0.1 broadcast_in_dim.8
  88.6 15.8 %all_to_all.28.refs_1_ = f32[16,18,8,128]{3,2,1,0:T(8,128)S(1)} all-to-all(f32[16,18,8,128]{3,2,1,0:T(8,128)S(1)} %broadcast_in_dim.8), channel_id=1, replica_groups=mesh['y'=4,'x'=4,'zh'=4,'zl'=4,'core'=2] {'y','x'}, dimensions={0} | all-to-all | bytes 2359296 | tf_op jit(solution)/shard_map/all_to_all | solution.py:250
  104.4 8.5 %collective-permute-start.1 = (f32[16,18,8,128]{3,2,1,0:T(8,128)S(1)}, f32[16,18,8,128]{3,2,1,0:T(8,128)S(1)}, u32[]{:S(2)}, u32[]{:S(2)}) collective-permute-start(f32[16,18,8,128]{3,2,1,0:T(8,128)S(1)} %all_to_all.28.refs_1_), channel_id=1, source_target_pairs={{0,1},{1,0},{2,3},{3,2},{4,5},{5,4},{6,7},{7,6},{8,9},{9,8},{10,11... | collective-permute-start | bytes 3538952 | tf_op jit(solution)/shard_map/ppermute | solution.py:251
  112.9 2.3 %collective-permute-done.1.refs_2_ = f32[16,18,8,128]{3,2,1,0:T(8,128)S(1)} collective-permute-done((f32[16,18,8,128]{3,2,1,0:T(8,128)S(1)}, f32[16,18,8,128]{3,2,1,0:T(8,128)S(1)}, u32[]{:S(2)}, u32[]{:S(2)}) %collective-permute-start.1) | collective-permute-done | bytes 1179680 | tf_op jit(solution)/shard_map/ppermute | solution.py:251
  115.2 31.6 %iterate.1 = (f32[64,128]{1,0:T(8,128)}, f32[16,8,256]{2,1,0:T(8,128)S(1)}) custom-call(s32[2]{0:T(128)S(1)} %pad_add_fusion.place_ref.refs_0_, f32[16,18,8,128]{3,2,1,0:T(8,128)S(1)} %all_to_all.28.refs_1_, f32[16,18,8,128]{3,2,1,0:T(8,128)S(1)} %collective-permute-done.1.refs_2_, bf16[1024,384]{1,0:T(8,128)(2,1)S(1)} %bitcast.16, ...), custom_call_target="tpu_custom_call" | custom-call | tf_op jit(solution)/shard_map/iterate/pallas_call | solution.py:253
  146.8 9.6 %all_to_all.29 = f32[16,8,256]{2,1,0:T(8,128)S(1)} all-to-all(f32[16,8,256]{2,1,0:T(8,128)S(1)} %get-tuple-element.5), channel_id=1, replica_groups=mesh['y'=4,'x'=4,'zh'=4,'zl'=4,'core'=2] {'y','x'}, dimensions={0} | all-to-all | bytes 262144 | tf_op jit(solution)/shard_map/all_to_all | solution.py:271
  156.4 0.7 copy.11
  (4 shorter events, 0.1 us)
Async XLA Ops:
  22.3 6.9 %collective-permute-start = (bf16[1024,384]{1,0:T(8,128)(2,1)S(1)}, bf16[1024,384]{1,0:T(8,128)(2,1)S(1)}, u32[]{:S(2)}, u32[]{:S(2)}) collective-permute-start(bf16[1024,384]{1,0:T(8,128)(2,1)S(1)} %bitcast.14), channel_id=1, source_target_pairs={{0,1},{1,0},{2,3},{3,2},{4,5},{5,4},{6,7},{7,6},{8,9},{9,8},{10,11... | collective-permute-start | bytes 2359304 | tf_op jit(solution)/shard_map/ppermute | solution.py:233
  104.4 10.8 %collective-permute-start.1 = (f32[16,18,8,128]{3,2,1,0:T(8,128)S(1)}, f32[16,18,8,128]{3,2,1,0:T(8,128)S(1)}, u32[]{:S(2)}, u32[]{:S(2)}) collective-permute-start(f32[16,18,8,128]{3,2,1,0:T(8,128)S(1)} %all_to_all.28.refs_1_), channel_id=1, source_target_pairs={{0,1},{1,0},{2,3},{3,2},{4,5},{5,4},{6,7},{7,6},{8,9},{9,8},{10,11... | collective-permute-start | bytes 3538952 | tf_op jit(solution)/shard_map/ppermute | solution.py:251

commit v4 on v3

--- a/solution.py
+++ b/solution.py
@@ -15,6 +15,8 @@
 LEAST_PIVOT = 2e-3
 CHUNK = 256
 MODE = ("y", "x")
+PLANES = ("y", "x", "z0")
+PAIR = HALF_BLOCKS // 2
 
 SLOTS = [(t, t + d) for t in range(4) for d in range(4)]
 
@@ -55,10 +57,10 @@
         return tile[(a % 2) * BLOCK : (a % 2 + 1) * BLOCK, (b % 2) * BLOCK : (b % 2 + 1) * BLOCK]
 
     for slot, (a, b) in enumerate(SLOTS):
-        out_ref[:, slot] = block(a, b).reshape(SPLIT, SLIVER, BLOCK)
+        out_ref[:, slot // PAIR, slot % PAIR] = block(a, b).reshape(SPLIT, SLIVER, BLOCK)
     for s in range(2):
         far = jnp.where(core == 0, block(s, s + 4), block(s + 2, s + 6))
-        out_ref[:, 16 + s] = far.reshape(SPLIT, SLIVER, BLOCK)
+        out_ref[:, 1, PAIR - 2 + s] = far.reshape(SPLIT, SLIVER, BLOCK)
 
 
 def inverse_factor(corr, inv_ref):
@@ -134,13 +136,13 @@
 
     for slot, (a, b) in enumerate(SLOTS):
         for ref, shift in ((own_ref, 0), (twin_ref, 4)):
-            value = ref[:, slot].reshape(BLOCK, BLOCK)
+            value = ref[:, slot // PAIR, slot % PAIR].reshape(BLOCK, BLOCK)
             if a == b:
                 largest = jnp.maximum(largest, jnp.where(diagonal, value, 0.0))
             put((a + shift) % 8, (b + shift) % 8, value)
     for s in range(2):
-        put(2 * core + s, 2 * core + s + 4, own_ref[:, 16 + s].reshape(BLOCK, BLOCK))
-        put(6 - 2 * core + s, 2 - 2 * core + s, twin_ref[:, 16 + s].reshape(BLOCK, BLOCK))
+        put(2 * core + s, 2 * core + s + 4, own_ref[:, 1, PAIR - 2 + s].reshape(BLOCK, BLOCK))
+        put(6 - 2 * core + s, 2 - 2 * core + s, twin_ref[:, 1, PAIR - 2 + s].reshape(BLOCK, BLOCK))
     scale = 1.0 / jnp.max(largest)
 
     def set_pair(side, rows, value):
@@ -233,21 +235,21 @@
     twin = lax.ppermute(own, "core", swap)
     partial_gram = pl.pallas_call(
         gram_kernel,
-        out_shape=jax.ShapeDtypeStruct((SPLIT, HALF_BLOCKS, SLIVER, BLOCK), jnp.float32),
+        out_shape=jax.ShapeDtypeStruct((SPLIT, 2, PAIR, SLIVER, BLOCK), jnp.float32),
         in_specs=[smem, vmem, vmem],
         out_specs=vmem,
         compiler_params=pltpu.CompilerParams(vmem_limit_bytes=16 * 1024 * 1024),
         name="gram",
     )(place, own, twin)
 
-    got = lax.all_to_all(partial_gram, MODE, split_axis=0, concat_axis=0, tiled=True)
+    partial_gram = partial_gram.reshape(2 * SPLIT, PAIR, SLIVER, BLOCK)
+    got = lax.all_to_all(partial_gram, PLANES, split_axis=0, concat_axis=0, tiled=True)
     sliver = jnp.sum(got, axis=0)
-    got = jnp.broadcast_to(sliver[None], (lax.axis_size("zl"),) + sliver.shape)
-    got = lax.all_to_all(got, "zl", split_axis=0, concat_axis=0, tiled=True)
-    got = lax.all_gather(jnp.sum(got, axis=0), "zh", axis=0, tiled=False)
-    sliver = jnp.sum(got, axis=0)
-    got = jnp.broadcast_to(sliver[None], (SPLIT,) + sliver.shape)
-    own_gram = lax.all_to_all(got, MODE, split_axis=0, concat_axis=0, tiled=True)
+    for axis in ("z1", "zh"):
+        sliver = jnp.sum(lax.all_gather(sliver, axis, axis=0, tiled=False), axis=0)
+    got = jnp.broadcast_to(sliver[None], got.shape)
+    own_gram = lax.all_to_all(got, PLANES, split_axis=0, concat_axis=0, tiled=True)
+    own_gram = own_gram.reshape(SPLIT, 2, PAIR, SLIVER, BLOCK)
     twin_gram = lax.ppermute(own_gram, "core", swap)
 
     basis, core_rows = pl.pallas_call(
@@ -273,8 +275,8 @@
 
 
 def solution(mesh):
-    chips = Mesh(mesh.devices.reshape(4, 4, 4, mesh.devices.shape[1] // 8, 2), ("y", "x", "zh", "zl", "core"))
-    rest = ("zh", "zl", "core")
+    chips = Mesh(mesh.devices.reshape(4, 4, mesh.devices.shape[1] // 8, 2, 2, 2), ("y", "x", "zh", "z1", "z0", "core"))
+    rest = ("zh", "z1", "z0", "core")
     in_specs = (P(MODE, rest), P(MODE, None))
     out_specs = (P(MODE, None), P(MODE, rest))
     return jax.shard_map(on_device, mesh=chips, in_specs=in_specs, out_specs=out_specs, check_vma=False)

time: 158 us -> 152 us (0.962)
  blocking collectives: 103 us -> 97.3 us
    all_to_all x3 -> x2, blocking collectives: 49.2 us -> 39.3 us  [the longest x1 22.6 us: on_device(): lax.all_to_all(partial_gram, PLANES, split_axis=0, concat_axis=0, tiled=T...]
    all_gather x1 -> x2, blocking collectives: 24.6 us -> 28.4 us  [on_device(): sliver = jnp.sum(lax.all_gather(sliver, axis, axis=0, tiled=False), axis=0)]
where the time goes in v4:
time: 152 us; the launch traced here: 151 us
  blocking collectives  97.3 us (64%)
  Pallas kernels  32.8 us (22%)
  starting transfers between devices  13.6 us (9%)
  waiting for transfers between devices  4.08 us (3%)
  local copies, waits for them, and re-layouts  1.86 us (1%)
    pallas_call x1, Pallas kernels, on_device(): pl.pallas_call(lambda *refs: iterate_kernel(cols, *refs), out_shape=(jax....  31.6 us
    all_gather x2, blocking collectives, on_device(): sliver = jnp.sum(lax.all_gather(sliver, axis, axis=0, tiled=False), axis=0)  28.4 us
    all_to_all x1, blocking collectives, on_device(): lax.all_to_all(partial_gram, PLANES, split_axis=0, concat_axis=0, tiled=T...  22.6 us
    all_to_all x1, blocking collectives, on_device(): lax.all_to_all(parts, MODE, split_axis=0, concat_axis=0, tiled=True)  19.6 us
    all_to_all x1, blocking collectives, on_device(): lax.all_to_all(got, PLANES, split_axis=0, concat_axis=0, tiled=True)  16.7 us
    all_to_all x1, blocking collectives, on_device(): lax.all_to_all(core_rows, MODE, split_axis=0, concat_axis=0, tiled=True)  9.95 us
    ppermute x1, starting transfers between devices, on_device(): twin_gram = lax.ppermute(own_gram, 'core', swap)  8.57 us
    ppermute x1, starting transfers between devices, on_device(): twin = lax.ppermute(own, 'core', swap)  5.01 us
  transfers between devices with their start and end apart: 2, of which 2 were waited for; matrix products, arithmetic and copies ran while one was open for 0% of the time, Pallas kernels for 0%

profile of v4, /device:TPU:1, one launch (start us, length us, event | category | flops | bytes accessed | tf_op | source)
XLA Modules:
  0.0 151.3 jit_solution(7467011209232563770)
XLA Ops:
  0.6 1.1 copy.8
  1.7 0.8 fusion
  2.6 0.1 pad_maximum_fusion
  2.6 19.6 %all_to_all.20 = bf16[16,64,384]{2,1,0:T(8,128)(2,1)S(1)} all-to-all(bf16[16,64,384]{2,1,0:T(8,128)(2,1)S(1)} %pad_maximum_fusion), channel_id=1, replica_groups=mesh['y'=4,'x'=4,'zh'=4,'z1'=2,'z0'=2,'core'=2] {'y','x'}, dimensions={0} | all-to-all | bytes 1572864 | tf_op jit(solution)/shard_map/all_to_all | solution.py:234
  22.3 5.0 %collective-permute-start = (bf16[1024,384]{1,0:T(8,128)(2,1)S(1)}, bf16[1024,384]{1,0:T(8,128)(2,1)S(1)}, u32[]{:S(2)}, u32[]{:S(2)}) collective-permute-start(bf16[1024,384]{1,0:T(8,128)(2,1)S(1)} %bitcast.17), channel_id=1, source_target_pairs={{0,1},{1,0},{2,3},{3,2},{4,5},{5,4},{6,7},{7,6},{8,9},{9,8},{10,11... | collective-permute-start | bytes 2359304 | tf_op jit(solution)/shard_map/ppermute | solution.py:235
  27.3 0.1 pad_add_fusion.place_ref.refs_0_
  27.4 1.8 %collective-permute-done.twin_ref.refs_4_ = bf16[1024,384]{1,0:T(8,128)(2,1)S(1)} collective-permute-done((bf16[1024,384]{1,0:T(8,128)(2,1)S(1)}, bf16[1024,384]{1,0:T(8,128)(2,1)S(1)}, u32[]{:S(2)}, u32[]{:S(2)}) %collective-permute-start) | collective-permute-done | bytes 786464 | tf_op jit(solution)/shard_map/ppermute | solution.py:235
  29.2 1.2 gram.1
  30.3 22.6 %all_to_all.21 = f32[32,9,8,128]{3,2,1,0:T(8,128)S(1)} all-to-all(f32[32,9,8,128]{3,2,1,0:T(8,128)S(1)} %bitcast.20), channel_id=1, replica_groups=mesh['y'=4,'x'=4,'zh'=4,'z1'=2,'z0'=2,'core'=2] {'y','x','z0'}, dimensions={0} | all-to-all | bytes 2359296 | tf_op jit(solution)/shard_map/all_to_all | solution.py:246
  52.9 0.1 reduce_sum.27
  53.0 5.4 %all-gather = f32[18,8,128]{2,1,0:T(8,128)S(1)} all-gather(f32[9,8,128]{2,1,0:T(8,128)S(1)} %reduce_sum.27), channel_id=2, replica_groups=mesh['y'=4,'x'=4,'zh'=4,'z1'=2,'z0'=2,'core'=2] {'z1'}, dimensions={0}, use_global_device_ids=true | all-gather | bytes 110592 | tf_op jit(solution)/shard_map/all_gather | solution.py:249
  58.4 23.0 %all-gather.1 = f32[36,8,128]{2,1,0:T(8,128)S(1)} all-gather(f32[9,8,128]{2,1,0:T(8,128)S(1)} %reduce_sum.28), channel_id=3, replica_groups=mesh['y'=4,'x'=4,'zh'=4,'z1'=2,'z0'=2,'core'=2] {'zh'}, dimensions={0}, use_global_device_ids=true | all-gather | bytes 184320 | tf_op jit(solution)/shard_map/all_gather | solution.py:249
  81.4 0.1 broadcast_in_dim.5
  81.5 16.7 %all_to_all.22 = f32[32,9,8,128]{3,2,1,0:T(8,128)S(1)} all-to-all(f32[32,9,8,128]{3,2,1,0:T(8,128)S(1)} %broadcast_in_dim.5), channel_id=1, replica_groups=mesh['y'=4,'x'=4,'zh'=4,'z1'=2,'z0'=2,'core'=2] {'y','x','z0'}, dimensions={0} | all-to-all | bytes 2359296 | tf_op jit(solution)/shard_map/all_to_all | solution.py:251
  98.2 8.6 %collective-permute-start.1 = (f32[16,2,9,8,128]{4,3,2,1,0:T(8,128)S(1)}, f32[16,2,9,8,128]{4,3,2,1,0:T(8,128)S(1)}, u32[]{:S(2)}, u32[]{:S(2)}) collective-permute-start(f32[16,2,9,8,128]{4,3,2,1,0:T(8,128)S(1)} %bitcast.21), channel_id=1, source_target_pairs={{0,1},{1,0},{2,3},{3,2},{4,5},{5,4},{6,7},{7,6},{8,9},{9,8},{10,11... | collective-permute-start | bytes 3538952 | tf_op jit(solution)/shard_map/ppermute | solution.py:253
  106.8 2.3 %collective-permute-done.1.refs_2_ = f32[16,2,9,8,128]{4,3,2,1,0:T(8,128)S(1)} collective-permute-done((f32[16,2,9,8,128]{4,3,2,1,0:T(8,128)S(1)}, f32[16,2,9,8,128]{4,3,2,1,0:T(8,128)S(1)}, u32[]{:S(2)}, u32[]{:S(2)}) %collective-permute-start.1) | collective-permute-done | bytes 1179680 | tf_op jit(solution)/shard_map/ppermute | solution.py:253
  109.1 31.6 %iterate.1 = (f32[64,128]{1,0:T(8,128)}, f32[16,8,256]{2,1,0:T(8,128)S(1)}) custom-call(s32[2]{0:T(128)S(1)} %pad_add_fusion.place_ref.refs_0_, f32[16,2,9,8,128]{4,3,2,1,0:T(8,128)S(1)} %bitcast.22, f32[16,2,9,8,128]{4,3,2,1,0:T(8,128)S(1)} %collective-permute-done.1.refs_2_, bf16[1024,384]{1,0:T(8,128)(2,1)S(1)} %bitcast.19, ...), custom_call_target="tpu_custom_call" | custom-call | tf_op jit(solution)/shard_map/iterate/pallas_call | solution.py:255
  140.7 10.0 %all_to_all.23 = f32[16,8,256]{2,1,0:T(8,128)S(1)} all-to-all(f32[16,8,256]{2,1,0:T(8,128)S(1)} %get-tuple-element.5), channel_id=1, replica_groups=mesh['y'=4,'x'=4,'zh'=4,'z1'=2,'z0'=2,'core'=2] {'y','x'}, dimensions={0} | all-to-all | bytes 262144 | tf_op jit(solution)/shard_map/all_to_all | solution.py:273
  150.7 0.7 copy.10
  (3 shorter events, 0.1 us)
Async XLA Ops:
  22.3 6.9 %collective-permute-start = (bf16[1024,384]{1,0:T(8,128)(2,1)S(1)}, bf16[1024,384]{1,0:T(8,128)(2,1)S(1)}, u32[]{:S(2)}, u32[]{:S(2)}) collective-permute-start(bf16[1024,384]{1,0:T(8,128)(2,1)S(1)} %bitcast.17), channel_id=1, source_target_pairs={{0,1},{1,0},{2,3},{3,2},{4,5},{5,4},{6,7},{7,6},{8,9},{9,8},{10,11... | collective-permute-start | bytes 2359304 | tf_op jit(solution)/shard_map/ppermute | solution.py:235
  98.2 10.8 %collective-permute-start.1 = (f32[16,2,9,8,128]{4,3,2,1,0:T(8,128)S(1)}, f32[16,2,9,8,128]{4,3,2,1,0:T(8,128)S(1)}, u32[]{:S(2)}, u32[]{:S(2)}) collective-permute-start(f32[16,2,9,8,128]{4,3,2,1,0:T(8,128)S(1)} %bitcast.21), channel_id=1, source_target_pairs={{0,1},{1,0},{2,3},{3,2},{4,5},{5,4},{6,7},{7,6},{8,9},{9,8},{10,11... | collective-permute-start | bytes 3538952 | tf_op jit(solution)/shard_map/ppermute | solution.py:253

commit v5 on v4

--- a/solution.py
+++ b/solution.py
@@ -17,6 +17,7 @@
 MODE = ("y", "x")
 PLANES = ("y", "x", "z0")
 PAIR = HALF_BLOCKS // 2
+HALF_TOP = 14.0
 
 SLOTS = [(t, t + d) for t in range(4) for d in range(4)]
 
@@ -56,11 +57,20 @@
         tile = tiles[a // 2, b // 2]
         return tile[(a % 2) * BLOCK : (a % 2 + 1) * BLOCK, (b % 2) * BLOCK : (b % 2 + 1) * BLOCK]
 
-    for slot, (a, b) in enumerate(SLOTS):
-        out_ref[:, slot // PAIR, slot % PAIR] = block(a, b).reshape(SPLIT, SLIVER, BLOCK)
-    for s in range(2):
-        far = jnp.where(core == 0, block(s, s + 4), block(s + 2, s + 6))
-        out_ref[:, 1, PAIR - 2 + s] = far.reshape(SPLIT, SLIVER, BLOCK)
+    blocks = [block(a, b) for a, b in SLOTS]
+    blocks += [jnp.where(core == 0, block(s, s + 4), block(s + 2, s + 6)) for s in range(2)]
+    largest = jnp.abs(blocks[0])
+    for value in blocks[1:]:
+        largest = jnp.maximum(largest, jnp.abs(value))
+    largest = jnp.maximum(jnp.max(largest, axis=(0, 1), keepdims=True), 1e-30)
+    power = jnp.round(jnp.log2(largest))
+    scale = jnp.exp2(HALF_TOP - power)
+    for slot, value in enumerate(blocks):
+        value = (value * scale).reshape(SPLIT, SLIVER, BLOCK)
+        out_ref[:, slot // PAIR, slot % PAIR] = value.astype(out_ref.dtype)
+    power = jnp.broadcast_to(power, (SPLIT, SLIVER, BLOCK))
+    for plane in range(2):
+        out_ref[:, plane, PAIR] = power.astype(out_ref.dtype)
 
 
 def inverse_factor(corr, inv_ref):
@@ -235,19 +245,20 @@
     twin = lax.ppermute(own, "core", swap)
     partial_gram = pl.pallas_call(
         gram_kernel,
-        out_shape=jax.ShapeDtypeStruct((SPLIT, 2, PAIR, SLIVER, BLOCK), jnp.float32),
+        out_shape=jax.ShapeDtypeStruct((SPLIT, 2, PAIR + 1, SLIVER, BLOCK), jnp.float32),
         in_specs=[smem, vmem, vmem],
         out_specs=vmem,
         compiler_params=pltpu.CompilerParams(vmem_limit_bytes=16 * 1024 * 1024),
         name="gram",
     )(place, own, twin)
 
-    partial_gram = partial_gram.reshape(2 * SPLIT, PAIR, SLIVER, BLOCK)
+    partial_gram = partial_gram.astype(jnp.float16).reshape(2 * SPLIT, (PAIR + 1) * SLIVER, BLOCK)
     got = lax.all_to_all(partial_gram, PLANES, split_axis=0, concat_axis=0, tiled=True)
-    sliver = jnp.sum(got, axis=0)
+    got = got.astype(jnp.float32).reshape(2 * SPLIT, PAIR + 1, SLIVER, BLOCK)
+    sliver = jnp.sum(got[:, :PAIR] * jnp.exp2(got[:, PAIR:] - HALF_TOP), axis=0)
     for axis in ("z1", "zh"):
         sliver = jnp.sum(lax.all_gather(sliver, axis, axis=0, tiled=False), axis=0)
-    got = jnp.broadcast_to(sliver[None], got.shape)
+    got = jnp.broadcast_to(sliver[None], (2 * SPLIT,) + sliver.shape)
     own_gram = lax.all_to_all(got, PLANES, split_axis=0, concat_axis=0, tiled=True)
     own_gram = own_gram.reshape(SPLIT, 2, PAIR, SLIVER, BLOCK)
     twin_gram = lax.ppermute(own_gram, "core", swap)

time: 152 us -> 146 us (0.961)
  blocking collectives: 97.3 us -> 90.4 us
    all_to_all x1, blocking collectives: 22.6 us -> 17 us  [on_device(): lax.all_to_all(partial_gram, PLANES, split_axis=0, concat_axis=0, tiled=T...]
where the time goes in v5:
time: 146 us
  blocking collectives  90.4 us (62%)
  Pallas kernels  33 us (23%)
  starting transfers between devices  14.3 us (10%)
  waiting for transfers between devices  4.08 us (3%)
  local copies, waits for them, and re-layouts  1.86 us (1%)
    pallas_call x1, Pallas kernels, on_device(): pl.pallas_call(lambda *refs: iterate_kernel(cols, *refs), out_shape=(jax....  31.6 us
    all_gather x2, blocking collectives, on_device(): sliver = jnp.sum(lax.all_gather(sliver, axis, axis=0, tiled=False), axis=0)  27.2 us
    all_to_all x1, blocking collectives, on_device(): lax.all_to_all(parts, MODE, split_axis=0, concat_axis=0, tiled=True)  19.6 us
    all_to_all x1, blocking collectives, on_device(): lax.all_to_all(partial_gram, PLANES, split_axis=0, concat_axis=0, tiled=T...  17 us
    all_to_all x1, blocking collectives, on_device(): lax.all_to_all(got, PLANES, split_axis=0, concat_axis=0, tiled=True)  16.7 us
    all_to_all x1, blocking collectives, on_device(): lax.all_to_all(core_rows, MODE, split_axis=0, concat_axis=0, tiled=True)  9.84 us
    ppermute x1, starting transfers between devices, on_device(): twin_gram = lax.ppermute(own_gram, 'core', swap)  9.3 us
    ppermute x1, starting transfers between devices, on_device(): twin = lax.ppermute(own, 'core', swap)  5.01 us
  transfers between devices with their start and end apart: 2, of which 2 were waited for; matrix products, arithmetic and copies ran while one was open for 0% of the time, Pallas kernels for 0%

profile of v5, /device:TPU:1, one launch (start us, length us, event | category | flops | bytes accessed | tf_op | source)
XLA Modules:
  0.0 145.7 jit_solution(290305516393031078)
XLA Ops:
  0.6 1.1 copy.8
  1.7 0.8 fusion.4
  2.6 0.1 pad_maximum_fusion
  2.6 19.6 %all_to_all.20 = bf16[16,64,384]{2,1,0:T(8,128)(2,1)S(1)} all-to-all(bf16[16,64,384]{2,1,0:T(8,128)(2,1)S(1)} %pad_maximum_fusion), channel_id=1, replica_groups=mesh['y'=4,'x'=4,'zh'=4,'z1'=2,'z0'=2,'core'=2] {'y','x'}, dimensions={0} | all-to-all | bytes 1572864 | tf_op jit(solution)/shard_map/all_to_all | solution.py:244
  22.3 5.0 %collective-permute-start = (bf16[1024,384]{1,0:T(8,128)(2,1)S(1)}, bf16[1024,384]{1,0:T(8,128)(2,1)S(1)}, u32[]{:S(2)}, u32[]{:S(2)}) collective-permute-start(bf16[1024,384]{1,0:T(8,128)(2,1)S(1)} %bitcast.22), channel_id=1, source_target_pairs={{0,1},{1,0},{2,3},{3,2},{4,5},{5,4},{6,7},{7,6},{8,9},{9,8},{10,11... | collective-permute-start | bytes 2359304 | tf_op jit(solution)/shard_map/ppermute | solution.py:245
  27.3 0.1 pad_add_fusion.place_ref.refs_0_
  27.4 1.8 %collective-permute-done.twin_ref.refs_4_ = bf16[1024,384]{1,0:T(8,128)(2,1)S(1)} collective-permute-done((bf16[1024,384]{1,0:T(8,128)(2,1)S(1)}, bf16[1024,384]{1,0:T(8,128)(2,1)S(1)}, u32[]{:S(2)}, u32[]{:S(2)}) %collective-permute-start) | collective-permute-done | bytes 786464 | tf_op jit(solution)/shard_map/ppermute | solution.py:245
  29.2 1.4 gram.1
  30.6 0.1 convert_element_type.8
  30.7 17.0 %all_to_all.21 = f16[32,80,128]{2,1,0:T(8,128)(2,1)S(1)} all-to-all(f16[32,80,128]{2,1,0:T(8,128)(2,1)S(1)} %bitcast.27), channel_id=1, replica_groups=mesh['y'=4,'x'=4,'zh'=4,'z1'=2,'z0'=2,'core'=2] {'y','x','z0'}, dimensions={0} | all-to-all | bytes 1310720 | tf_op jit(solution)/shard_map/all_to_all | solution.py:256
  47.7 0.1 bitcast_convert_fusion
  47.8 0.1 fusion
  47.9 5.2 %all-gather = f32[18,8,128]{2,1,0:T(8,128)S(1)} all-gather(f32[9,8,128]{2,1,0:T(8,128)S(1)} %fusion), channel_id=2, replica_groups=mesh['y'=4,'x'=4,'zh'=4,'z1'=2,'z0'=2,'core'=2] {'z1'}, dimensions={0}, use_global_device_ids=true | all-gather | bytes 110592 | tf_op jit(solution)/shard_map/all_gather | solution.py:260
  53.1 22.0 %all-gather.1 = f32[36,8,128]{2,1,0:T(8,128)S(1)} all-gather(f32[9,8,128]{2,1,0:T(8,128)S(1)} %reduce_sum.28), channel_id=3, replica_groups=mesh['y'=4,'x'=4,'zh'=4,'z1'=2,'z0'=2,'core'=2] {'zh'}, dimensions={0}, use_global_device_ids=true | all-gather | bytes 184320 | tf_op jit(solution)/shard_map/all_gather | solution.py:260
  75.2 0.1 broadcast_in_dim.5
  75.3 16.7 %all_to_all.22 = f32[32,9,8,128]{3,2,1,0:T(8,128)S(1)} all-to-all(f32[32,9,8,128]{3,2,1,0:T(8,128)S(1)} %broadcast_in_dim.5), channel_id=1, replica_groups=mesh['y'=4,'x'=4,'zh'=4,'z1'=2,'z0'=2,'core'=2] {'y','x','z0'}, dimensions={0} | all-to-all | bytes 2359296 | tf_op jit(solution)/shard_map/all_to_all | solution.py:262
  92.0 9.3 %collective-permute-start.1 = (f32[16,2,9,8,128]{4,3,2,1,0:T(8,128)S(1)}, f32[16,2,9,8,128]{4,3,2,1,0:T(8,128)S(1)}, u32[]{:S(2)}, u32[]{:S(2)}) collective-permute-start(f32[16,2,9,8,128]{4,3,2,1,0:T(8,128)S(1)} %bitcast.25), channel_id=1, source_target_pairs={{0,1},{1,0},{2,3},{3,2},{4,5},{5,4},{6,7},{7,6},{8,9},{9,8},{10,11... | collective-permute-start | bytes 3538952 | tf_op jit(solution)/shard_map/ppermute | solution.py:264
  101.3 2.3 %collective-permute-done.1.refs_2_ = f32[16,2,9,8,128]{4,3,2,1,0:T(8,128)S(1)} collective-permute-done((f32[16,2,9,8,128]{4,3,2,1,0:T(8,128)S(1)}, f32[16,2,9,8,128]{4,3,2,1,0:T(8,128)S(1)}, u32[]{:S(2)}, u32[]{:S(2)}) %collective-permute-start.1) | collective-permute-done | bytes 1179680 | tf_op jit(solution)/shard_map/ppermute | solution.py:264
  103.6 31.6 %iterate.1 = (f32[64,128]{1,0:T(8,128)}, f32[16,8,256]{2,1,0:T(8,128)S(1)}) custom-call(s32[2]{0:T(128)S(1)} %pad_add_fusion.place_ref.refs_0_, f32[16,2,9,8,128]{4,3,2,1,0:T(8,128)S(1)} %bitcast.26, f32[16,2,9,8,128]{4,3,2,1,0:T(8,128)S(1)} %collective-permute-done.1.refs_2_, bf16[1024,384]{1,0:T(8,128)(2,1)S(1)} %bitcast.24, ...), custom_call_target="tpu_custom_call" | custom-call | tf_op jit(solution)/shard_map/iterate/pallas_call | solution.py:266
  135.2 9.8 %all_to_all.23 = f32[16,8,256]{2,1,0:T(8,128)S(1)} all-to-all(f32[16,8,256]{2,1,0:T(8,128)S(1)} %get-tuple-element.5), channel_id=1, replica_groups=mesh['y'=4,'x'=4,'zh'=4,'z1'=2,'z0'=2,'core'=2] {'y','x'}, dimensions={0} | all-to-all | bytes 262144 | tf_op jit(solution)/shard_map/all_to_all | solution.py:284
  145.1 0.7 copy.10
  (4 shorter events, 0.1 us)
Async XLA Ops:
  22.3 6.9 %collective-permute-start = (bf16[1024,384]{1,0:T(8,128)(2,1)S(1)}, bf16[1024,384]{1,0:T(8,128)(2,1)S(1)}, u32[]{:S(2)}, u32[]{:S(2)}) collective-permute-start(bf16[1024,384]{1,0:T(8,128)(2,1)S(1)} %bitcast.22), channel_id=1, source_target_pairs={{0,1},{1,0},{2,3},{3,2},{4,5},{5,4},{6,7},{7,6},{8,9},{9,8},{10,11... | collective-permute-start | bytes 2359304 | tf_op jit(solution)/shard_map/ppermute | solution.py:245
  92.0 11.6 %collective-permute-start.1 = (f32[16,2,9,8,128]{4,3,2,1,0:T(8,128)S(1)}, f32[16,2,9,8,128]{4,3,2,1,0:T(8,128)S(1)}, u32[]{:S(2)}, u32[]{:S(2)}) collective-permute-start(f32[16,2,9,8,128]{4,3,2,1,0:T(8,128)S(1)} %bitcast.25), channel_id=1, source_target_pairs={{0,1},{1,0},{2,3},{3,2},{4,5},{5,4},{6,7},{7,6},{8,9},{9,8},{10,11... | collective-permute-start | bytes 3538952 | tf_op jit(solution)/shard_map/ppermute | solution.py:264

commit v6 on v5

--- a/solution.py
+++ b/solution.py
@@ -17,6 +17,7 @@
 MODE = ("y", "x")
 PLANES = ("y", "x", "z0")
 PAIR = HALF_BLOCKS // 2
+SHARE = ROWS // SPLIT // 4
 HALF_TOP = 14.0
 
 SLOTS = [(t, t + d) for t in range(4) for d in range(4)]
@@ -39,13 +40,14 @@
     return jnp.dot(left, right, preferred_element_type=jnp.float32)
 
 
-def gram_kernel(place_ref, own_ref, twin_ref, out_ref):
-    core = place_ref[0]
-    cols = own_ref.shape[1] - RANK
+def gram_kernel(place_ref, own_ref, twin_ref, initial_ref, out_ref, share_ref):
+    core, quarter = place_ref[0], place_ref[2]
+    rows_sent = pl.ds(pl.multiple_of(quarter * SHARE, SHARE), SHARE)
+    share_ref[...] = initial_ref[rows_sent, :].reshape(share_ref.shape)
 
     def rows(ref, a):
         start = pl.multiple_of(lax.rem(core * 512 + a * 256, ROWS), 256)
-        return ref[pl.ds(start, 256), :cols]
+        return ref[pl.ds(start, 256), :]
 
     own = [rows(own_ref, a) for a in range(4)]
     twin = [rows(twin_ref, a) for a in range(4)]
@@ -77,16 +79,16 @@
     panels = RANK // 8
     row = lax.broadcasted_iota(jnp.int32, (8, RANK), 0)
     lane = lax.broadcasted_iota(jnp.int32, (8, RANK), 1)
-    left = [corr[8 * p : 8 * p + 8, :] for p in range(panels)]
-    right = [jnp.where(lane == row + 8 * p, 1.0, 0.0) for p in range(panels)]
+    rows = [corr[8 * p : 8 * p + 8, :] for p in range(panels)]
     least = jnp.full((8, RANK), jnp.inf, jnp.float32)
 
     def columns_of(value, p):
         return [jnp.broadcast_to(value[:, 8 * p + k : 8 * p + k + 1], (8, RANK)) for k in range(8)]
 
     for p in range(panels):
-        here, there = left[p], right[p]
-        column = columns_of(here, p)
+        inside = jnp.logical_and(lane >= 8 * p, lane < 8 * p + 8)
+        column = columns_of(rows[p], p)
+        here = jnp.where(inside, jnp.where(lane == row + 8 * p, 1.0, 0.0), rows[p])
         pivots = jnp.zeros((8, RANK), jnp.float32)
         steps = []
         for k in range(0, 8, 2):
@@ -107,25 +109,25 @@
             tops = [heads(column[later]) for later in range(k + 2, 8)]
             for later, (one, two) in zip(range(k + 2, 8), tops):
                 column[later] = column[later] - lower * one - lowest * two
-            sides = heads(here), heads(there)
-            here = here - lower * sides[0][0] - lowest * sides[0][1]
-            there = there - lower * sides[1][0] - lowest * sides[1][1]
-            steps.append((k, ratio, tops, sides))
+            side = heads(here)
+            here = here - lower * side[0] - lowest * side[1]
+            steps.append((k, ratio, tops, side))
         least = jnp.minimum(least, pivots)
-        inv_ref[8 * p : 8 * p + 8, :] = there * lax.rsqrt(pivots)
+        inv_ref[8 * p : 8 * p + 8, :] = jnp.where(lane < 8 * p + 8, here * lax.rsqrt(pivots), 0.0)
         for q in range(p + 1, panels):
-            column = columns_of(left[q], p)
-            for k, ratio, tops, sides in steps:
+            column = columns_of(rows[q], p)
+            value = jnp.where(inside, 0.0, rows[q])
+            for k, ratio, tops, side in steps:
                 lower = column[k]
                 lowest = column[k + 1] - lower * ratio
                 for later, (one, two) in zip(range(k + 2, 8), tops):
                     column[later] = column[later] - lower * one - lowest * two
-                left[q] = left[q] - lower * sides[0][0] - lowest * sides[0][1]
-                right[q] = right[q] - lower * sides[1][0] - lowest * sides[1][1]
+                value = value - lower * side[0] - lowest * side[1]
+            rows[q] = value
     return jnp.min(least)
 
 
-def iterate_kernel(cols, place_ref, own_ref, twin_ref, field_ref, twin_field_ref, basis_ref, core_ref,
+def iterate_kernel(place_ref, own_ref, twin_ref, field_ref, basis_ref, core_ref,
                    high_ref, low_ref, pair_ref, image_ref, inv_ref):
     core, mode = place_ref[0], place_ref[1]
     row = lax.broadcasted_iota(jnp.int32, (RANK, RANK), 0)
@@ -161,13 +163,12 @@
         pair_ref[side, rows, RANK:] = low
 
     def start():
-        for half in range(2):
-            offset = pl.multiple_of(lax.rem(core * 512 + half * 512, ROWS), 512)
-            rows = pl.ds(half * 512, 512)
-            first = field_ref[pl.ds(offset, 512), cols:]
-            second = twin_field_ref[pl.ds(offset, 512), cols:]
-            pair_ref[0, rows, :RANK] = jnp.where(core == 0, first, second)
-            pair_ref[0, rows, RANK:] = jnp.where(core == 0, second, first)
+        for m in range(SPLIT):
+            for plane in range(2):
+                for ref, part in ((own_ref, core), (twin_ref, 1 - core)):
+                    begin = m * (ROWS // SPLIT) + plane * 2 * SHARE + part * SHARE - core * 512 + ROWS
+                    rows = pl.ds(pl.multiple_of(lax.rem(begin, ROWS), SHARE), SHARE)
+                    set_pair(0, rows, ref[m, plane, PAIR:].reshape(SHARE, RANK))
 
     def multiply(side):
         for r in range(ROWS // CHUNK):
@@ -217,40 +218,35 @@
 
     own_rows = ROWS // SPLIT
     basis_ref[...] = image_ref[pl.ds(pl.multiple_of(lax.rem(mode * own_rows + core * 512, ROWS), own_rows), own_rows), :]
-    total = jnp.zeros((RANK, cols), jnp.float32)
+    total = jnp.zeros((RANK, field_ref.shape[1]), jnp.float32)
     for half in range(2):
         offset = pl.multiple_of(lax.rem(core * 512 + half * 512, ROWS), 512)
-        total = total + dot_tn(pair_ref[0, pl.ds(half * 512, 512), :RANK], field_ref[pl.ds(offset, 512), :cols])
+        total = total + dot_tn(pair_ref[0, pl.ds(half * 512, 512), :RANK], field_ref[pl.ds(offset, 512), :])
     core_ref[...] = total.reshape(core_ref.shape)
 
 
 def on_device(unfolded, initial):
     held, cols = unfolded.shape[0], unfolded.shape[1] // SPLIT
     core, mode = lax.axis_index("core"), lax.axis_index(MODE)
-    place = jnp.stack([core, mode]).astype(jnp.int32)
+    place = jnp.stack([core, mode, 2 * lax.axis_index("z0") + core]).astype(jnp.int32)
     vmem = pl.BlockSpec(memory_space=pltpu.VMEM)
     smem = pl.BlockSpec(memory_space=pltpu.SMEM)
     swap = [(0, 1), (1, 0)]
 
-    high = lax.reduce_precision(initial, exponent_bits=8, mantissa_bits=7)
-    half = jnp.where(core == 0, high, initial - high).astype(jnp.bfloat16)
-    parts = jnp.concatenate(
-        [
-            unfolded.reshape(held, SPLIT, cols).transpose(1, 0, 2),
-            jnp.broadcast_to(half[None], (SPLIT, held, RANK)),
-        ],
-        axis=2,
-    )
-    own = lax.all_to_all(parts, MODE, split_axis=0, concat_axis=0, tiled=True).reshape(ROWS, cols + RANK)
+    parts = unfolded.reshape(held, SPLIT, cols).transpose(1, 0, 2)
+    own = lax.all_to_all(parts, MODE, split_axis=0, concat_axis=0, tiled=True).reshape(ROWS, cols)
     twin = lax.ppermute(own, "core", swap)
-    partial_gram = pl.pallas_call(
+    partial_gram, share = pl.pallas_call(
         gram_kernel,
-        out_shape=jax.ShapeDtypeStruct((SPLIT, 2, PAIR + 1, SLIVER, BLOCK), jnp.float32),
-        in_specs=[smem, vmem, vmem],
-        out_specs=vmem,
+        out_shape=(
+            jax.ShapeDtypeStruct((SPLIT, 2, PAIR + 1, SLIVER, BLOCK), jnp.float32),
+            jax.ShapeDtypeStruct((SHARE // SLIVER, SLIVER, RANK), jnp.float32),
+        ),
+        in_specs=[smem, vmem, vmem, vmem],
+        out_specs=(vmem, vmem),
         compiler_params=pltpu.CompilerParams(vmem_limit_bytes=16 * 1024 * 1024),
         name="gram",
-    )(place, own, twin)
+    )(place, own, twin, initial)
 
     partial_gram = partial_gram.astype(jnp.float16).reshape(2 * SPLIT, (PAIR + 1) * SLIVER, BLOCK)
     got = lax.all_to_all(partial_gram, PLANES, split_axis=0, concat_axis=0, tiled=True)
@@ -258,18 +254,19 @@
     sliver = jnp.sum(got[:, :PAIR] * jnp.exp2(got[:, PAIR:] - HALF_TOP), axis=0)
     for axis in ("z1", "zh"):
         sliver = jnp.sum(lax.all_gather(sliver, axis, axis=0, tiled=False), axis=0)
+    sliver = jnp.concatenate([sliver, share], axis=0)
     got = jnp.broadcast_to(sliver[None], (2 * SPLIT,) + sliver.shape)
     own_gram = lax.all_to_all(got, PLANES, split_axis=0, concat_axis=0, tiled=True)
-    own_gram = own_gram.reshape(SPLIT, 2, PAIR, SLIVER, BLOCK)
+    own_gram = own_gram.reshape((SPLIT, 2) + sliver.shape)
     twin_gram = lax.ppermute(own_gram, "core", swap)
 
     basis, core_rows = pl.pallas_call(
-        lambda *refs: iterate_kernel(cols, *refs),
+        iterate_kernel,
         out_shape=(
             jax.ShapeDtypeStruct((held, RANK), jnp.float32),
             jax.ShapeDtypeStruct((SPLIT, RANK // SPLIT, cols), jnp.float32),
         ),
-        in_specs=[smem, vmem, vmem, vmem, vmem],
+        in_specs=[smem, vmem, vmem, vmem],
         out_specs=(vmem, vmem),
         scratch_shapes=[
             pltpu.VMEM((ROWS, ROWS), jnp.bfloat16),
@@ -280,7 +277,7 @@
         ],
         compiler_params=pltpu.CompilerParams(vmem_limit_bytes=32 * 1024 * 1024),
         name="iterate",
-    )(place, own_gram, twin_gram, own, twin)
+    )(place, own_gram, twin_gram, own)
     core_cols = lax.all_to_all(core_rows, MODE, split_axis=0, concat_axis=0, tiled=True)
     return basis, core_cols.transpose(1, 0, 2).reshape(RANK // SPLIT, SPLIT * cols)
 

time: 146 us -> 145 us (level)
    all_to_all x1, blocking collectives: 16.7 us -> 19.7 us  [on_device(): lax.all_to_all(got, PLANES, split_axis=0, concat_axis=0, tiled=True)]
    all_to_all x1, blocking collectives: 19.6 us -> 16.9 us  [on_device(): lax.all_to_all(parts, MODE, split_axis=0, concat_axis=0, tiled=True)]
where the time goes in v6:
time: 145 us; the launch traced here: 144 us
  blocking collectives  90.7 us (63%)
  Pallas kernels  32.9 us (23%)
  starting transfers between devices  13.8 us (10%)
  waiting for transfers between devices  4.07 us (3%)
  local copies, waits for them, and re-layouts  1.85 us (1%)
    pallas_call x1, Pallas kernels, on_device(): pl.pallas_call(iterate_kernel, out_shape=(jax.ShapeDtypeStruct((held, RAN...  31.4 us
    all_gather x2, blocking collectives, on_device(): sliver = jnp.sum(lax.all_gather(sliver, axis, axis=0, tiled=False), axis=0)  27.3 us
    all_to_all x1, blocking collectives, on_device(): lax.all_to_all(got, PLANES, split_axis=0, concat_axis=0, tiled=True)  19.7 us
    all_to_all x1, blocking collectives, on_device(): lax.all_to_all(partial_gram, PLANES, split_axis=0, concat_axis=0, tiled=T...  17 us
    all_to_all x1, blocking collectives, on_device(): lax.all_to_all(parts, MODE, split_axis=0, concat_axis=0, tiled=True)  16.9 us
    all_to_all x1, blocking collectives, on_device(): lax.all_to_all(core_rows, MODE, split_axis=0, concat_axis=0, tiled=True)  9.79 us
    ppermute x1, starting transfers between devices, on_device(): twin_gram = lax.ppermute(own_gram, 'core', swap)  8.86 us
    ppermute x1, starting transfers between devices, on_device(): twin = lax.ppermute(own, 'core', swap)  4.92 us
  transfers between devices with their start and end apart: 2, of which 2 were waited for; matrix products, arithmetic and copies ran while one was open for 0% of the time, Pallas kernels for 0%

profile of v6, /device:TPU:1, one launch (start us, length us, event | category | flops | bytes accessed | tf_op | source)
XLA Modules:
  0.0 144.4 jit_solution(15865695958897309267)
XLA Ops:
  0.6 0.0 copy-start
  0.6 1.1 copy.8
  1.7 16.9 %all_to_all.20 = bf16[16,64,256]{2,1,0:T(8,128)(2,1)S(1)} all-to-all(bf16[16,64,256]{2,1,0:T(8,128)(2,1)S(1)} %bitcast.29), channel_id=1, replica_groups=mesh['y'=4,'x'=4,'zh'=4,'z1'=2,'z0'=2,'core'=2] {'y','x'}, dimensions={0} | all-to-all | bytes 1048576 | tf_op jit(solution)/shard_map/all_to_all | solution.py:237
  18.6 4.9 %collective-permute-start = (bf16[1024,256]{1,0:T(8,128)(2,1)S(1)}, bf16[1024,256]{1,0:T(8,128)(2,1)S(1)}, u32[]{:S(2)}, u32[]{:S(2)}) collective-permute-start(bf16[1024,256]{1,0:T(8,128)(2,1)S(1)} %bitcast.25), channel_id=1, source_target_pairs={{0,1},{1,0},{2,3},{3,2},{4,5},{5,4},{6,7},{7,6},{8,9},{9,8},{10,11... | collective-permute-start | bytes 1572872 | tf_op jit(solution)/shard_map/ppermute | solution.py:238
  23.6 0.1 pad_add_fusion.place_ref
  23.6 1.4 collective-permute-done.twin_ref
  25.1 0.0 copy-done
  25.1 1.4 gram.1
  26.5 0.1 convert_element_type.4
  26.6 17.0 %all_to_all.21 = f16[32,80,128]{2,1,0:T(8,128)(2,1)S(1)} all-to-all(f16[32,80,128]{2,1,0:T(8,128)(2,1)S(1)} %bitcast.28), channel_id=1, replica_groups=mesh['y'=4,'x'=4,'zh'=4,'z1'=2,'z0'=2,'core'=2] {'y','x','z0'}, dimensions={0} | all-to-all | bytes 1310720 | tf_op jit(solution)/shard_map/all_to_all | solution.py:252
  43.6 0.1 bitcast_convert_fusion
  43.8 0.1 fusion
  43.9 5.2 %all-gather = f32[18,8,128]{2,1,0:T(8,128)S(1)} all-gather(f32[9,8,128]{2,1,0:T(8,128)S(1)} %fusion), channel_id=2, replica_groups=mesh['y'=4,'x'=4,'zh'=4,'z1'=2,'z0'=2,'core'=2] {'z1'}, dimensions={0}, use_global_device_ids=true | all-gather | bytes 110592 | tf_op jit(solution)/shard_map/all_gather | solution.py:256
  49.1 22.0 %all-gather.1 = f32[36,8,128]{2,1,0:T(8,128)S(1)} all-gather(f32[9,8,128]{2,1,0:T(8,128)S(1)} %reduce_sum.28), channel_id=3, replica_groups=mesh['y'=4,'x'=4,'zh'=4,'z1'=2,'z0'=2,'core'=2] {'zh'}, dimensions={0}, use_global_device_ids=true | all-gather | bytes 184320 | tf_op jit(solution)/shard_map/all_gather | solution.py:256
  71.2 0.1 broadcast_in_dim.2
  71.3 19.7 %all_to_all.22 = f32[32,11,8,128]{3,2,1,0:T(8,128)S(1)} all-to-all(f32[32,11,8,128]{3,2,1,0:T(8,128)S(1)} %broadcast_in_dim.2), channel_id=1, replica_groups=mesh['y'=4,'x'=4,'zh'=4,'z1'=2,'z0'=2,'core'=2] {'y','x','z0'}, dimensions={0} | all-to-all | bytes 2883584 | tf_op jit(solution)/shard_map/all_to_all | solution.py:259
  91.0 8.9 %collective-permute-start.1 = (f32[16,2,11,8,128]{4,3,2,1,0:T(8,128)S(1)}, f32[16,2,11,8,128]{4,3,2,1,0:T(8,128)S(1)}, u32[]{:S(2)}, u32[]{:S(2)}) collective-permute-start(f32[16,2,11,8,128]{4,3,2,1,0:T(8,128)S(1)} %bitcast.23), channel_id=1, source_target_pairs={{0,1},{1,0},{2,3},{3,2},{4,5},{5,4},{6,7},{7,6},{8,9},{9,8},{10,11... | collective-permute-start | bytes 4325384 | tf_op jit(solution)/shard_map/ppermute | solution.py:261
  99.9 2.6 %collective-permute-done.1.twin_ref = f32[16,2,11,8,128]{4,3,2,1,0:T(8,128)S(1)} collective-permute-done((f32[16,2,11,8,128]{4,3,2,1,0:T(8,128)S(1)}, f32[16,2,11,8,128]{4,3,2,1,0:T(8,128)S(1)}, u32[]{:S(2)}, u32[]{:S(2)}) %collective-permute-start.1) | collective-permute-done | bytes 1441824 | tf_op jit(solution)/shard_map/ppermute | solution.py:261
  102.5 31.4 %iterate.1 = (f32[64,128]{1,0:T(8,128)}, f32[16,8,256]{2,1,0:T(8,128)S(1)}) custom-call(s32[3]{0:T(128)S(1)} %pad_add_fusion.place_ref, f32[16,2,11,8,128]{4,3,2,1,0:T(8,128)S(1)} %bitcast.24, f32[16,2,11,8,128]{4,3,2,1,0:T(8,128)S(1)} %collective-permute-done.1.twin_ref, bf16[1024,256]{1,0:T(8,128)(2,1)S(1)} %bitcast.27), custom_call_target="tpu_custom_call" | custom-call | tf_op jit(solution)/shard_map/iterate/pallas_call | solution.py:263
  134.0 9.8 %all_to_all.23 = f32[16,8,256]{2,1,0:T(8,128)S(1)} all-to-all(f32[16,8,256]{2,1,0:T(8,128)S(1)} %get-tuple-element.9), channel_id=1, replica_groups=mesh['y'=4,'x'=4,'zh'=4,'z1'=2,'z0'=2,'core'=2] {'y','x'}, dimensions={0} | all-to-all | bytes 262144 | tf_op jit(solution)/shard_map/all_to_all | solution.py:281
  143.7 0.7 copy.10
  (4 shorter events, 0.1 us)
Async XLA Ops:
  0.6 24.4 %copy-start = (f32[64,128]{1,0:T(8,128)S(1)}, f32[64,128]{1,0:T(8,128)}, u32[]{:S(2)}) copy-start(f32[64,128]{1,0:T(8,128)} %initial_ref.1) | copy-start | bytes 98308
  18.6 6.4 %collective-permute-start = (bf16[1024,256]{1,0:T(8,128)(2,1)S(1)}, bf16[1024,256]{1,0:T(8,128)(2,1)S(1)}, u32[]{:S(2)}, u32[]{:S(2)}) collective-permute-start(bf16[1024,256]{1,0:T(8,128)(2,1)S(1)} %bitcast.25), channel_id=1, source_target_pairs={{0,1},{1,0},{2,3},{3,2},{4,5},{5,4},{6,7},{7,6},{8,9},{9,8},{10,11... | collective-permute-start | bytes 1572872 | tf_op jit(solution)/shard_map/ppermute | solution.py:238
  91.0 11.5 %collective-permute-start.1 = (f32[16,2,11,8,128]{4,3,2,1,0:T(8,128)S(1)}, f32[16,2,11,8,128]{4,3,2,1,0:T(8,128)S(1)}, u32[]{:S(2)}, u32[]{:S(2)}) collective-permute-start(f32[16,2,11,8,128]{4,3,2,1,0:T(8,128)S(1)} %bitcast.23), channel_id=1, source_target_pairs={{0,1},{1,0},{2,3},{3,2},{4,5},{5,4},{6,7},{7,6},{8,9},{9,8},{10,11... | collective-permute-start | bytes 4325384 | tf_op jit(solution)/shard_map/ppermute | solution.py:261

commit v7 on v6

--- a/solution.py
+++ b/solution.py
@@ -12,10 +12,10 @@
 HALF_BLOCKS = 18
 SPLIT = 16
 SLIVER = BLOCK // SPLIT
-LEAST_PIVOT = 2e-3
+LEAST_PIVOT = 5e-3
 CHUNK = 256
 MODE = ("y", "x")
-PLANES = ("y", "x", "z0")
+PLANES = ("z0", "y", "x")
 PAIR = HALF_BLOCKS // 2
 SHARE = ROWS // SPLIT // 4
 HALF_TOP = 14.0
@@ -69,10 +69,10 @@
     scale = jnp.exp2(HALF_TOP - power)
     for slot, value in enumerate(blocks):
         value = (value * scale).reshape(SPLIT, SLIVER, BLOCK)
-        out_ref[:, slot // PAIR, slot % PAIR] = value.astype(out_ref.dtype)
+        out_ref[slot // PAIR, :, slot % PAIR] = value.astype(out_ref.dtype)
     power = jnp.broadcast_to(power, (SPLIT, SLIVER, BLOCK))
     for plane in range(2):
-        out_ref[:, plane, PAIR] = power.astype(out_ref.dtype)
+        out_ref[plane, :, PAIR] = power.astype(out_ref.dtype)
 
 
 def inverse_factor(corr, inv_ref):
@@ -148,13 +148,13 @@
 
     for slot, (a, b) in enumerate(SLOTS):
         for ref, shift in ((own_ref, 0), (twin_ref, 4)):
-            value = ref[:, slot // PAIR, slot % PAIR].reshape(BLOCK, BLOCK)
+            value = ref[slot // PAIR, :, slot % PAIR].reshape(BLOCK, BLOCK)
             if a == b:
                 largest = jnp.maximum(largest, jnp.where(diagonal, value, 0.0))
             put((a + shift) % 8, (b + shift) % 8, value)
     for s in range(2):
-        put(2 * core + s, 2 * core + s + 4, own_ref[:, 1, PAIR - 2 + s].reshape(BLOCK, BLOCK))
-        put(6 - 2 * core + s, 2 - 2 * core + s, twin_ref[:, 1, PAIR - 2 + s].reshape(BLOCK, BLOCK))
+        put(2 * core + s, 2 * core + s + 4, own_ref[1, :, PAIR - 2 + s].reshape(BLOCK, BLOCK))
+        put(6 - 2 * core + s, 2 - 2 * core + s, twin_ref[1, :, PAIR - 2 + s].reshape(BLOCK, BLOCK))
     scale = 1.0 / jnp.max(largest)
 
     def set_pair(side, rows, value):
@@ -168,7 +168,7 @@
                 for ref, part in ((own_ref, core), (twin_ref, 1 - core)):
                     begin = m * (ROWS // SPLIT) + plane * 2 * SHARE + part * SHARE - core * 512 + ROWS
                     rows = pl.ds(pl.multiple_of(lax.rem(begin, ROWS), SHARE), SHARE)
-                    set_pair(0, rows, ref[m, plane, PAIR:].reshape(SHARE, RANK))
+                    set_pair(0, rows, ref[plane, m, PAIR:].reshape(SHARE, RANK))
 
     def multiply(side):
         for r in range(ROWS // CHUNK):
@@ -239,7 +239,7 @@
     partial_gram, share = pl.pallas_call(
         gram_kernel,
         out_shape=(
-            jax.ShapeDtypeStruct((SPLIT, 2, PAIR + 1, SLIVER, BLOCK), jnp.float32),
+            jax.ShapeDtypeStruct((2, SPLIT, PAIR + 1, SLIVER, BLOCK), jnp.float32),
             jax.ShapeDtypeStruct((SHARE // SLIVER, SLIVER, RANK), jnp.float32),
         ),
         in_specs=[smem, vmem, vmem, vmem],
@@ -257,7 +257,7 @@
     sliver = jnp.concatenate([sliver, share], axis=0)
     got = jnp.broadcast_to(sliver[None], (2 * SPLIT,) + sliver.shape)
     own_gram = lax.all_to_all(got, PLANES, split_axis=0, concat_axis=0, tiled=True)
-    own_gram = own_gram.reshape((SPLIT, 2) + sliver.shape)
+    own_gram = own_gram.reshape((2, SPLIT) + sliver.shape)
     twin_gram = lax.ppermute(own_gram, "core", swap)
 
     basis, core_rows = pl.pallas_call(

time: 145 us -> 144 us (level)
    all_to_all x1, blocking collectives: 17 us -> 15.4 us  [on_device(): lax.all_to_all(partial_gram, PLANES, split_axis=0, concat_axis=0, tiled=T...]
where the time goes in v7:
time: 144 us
  blocking collectives  89.4 us (62%)
  Pallas kernels  32.8 us (23%)
  starting transfers between devices  14.6 us (10%)
  waiting for transfers between devices  4.07 us (3%)
  local copies, waits for them, and re-layouts  1.85 us (1%)
    pallas_call x1, Pallas kernels, on_device(): pl.pallas_call(iterate_kernel, out_shape=(jax.ShapeDtypeStruct((held, RAN...  31.4 us
    all_gather x2, blocking collectives, on_device(): sliver = jnp.sum(lax.all_gather(sliver, axis, axis=0, tiled=False), axis=0)  27 us
    all_to_all x1, blocking collectives, on_device(): lax.all_to_all(got, PLANES, split_axis=0, concat_axis=0, tiled=True)  20.1 us
    all_to_all x1, blocking collectives, on_device(): lax.all_to_all(parts, MODE, split_axis=0, concat_axis=0, tiled=True)  16.9 us
    all_to_all x1, blocking collectives, on_device(): lax.all_to_all(partial_gram, PLANES, split_axis=0, concat_axis=0, tiled=T...  15.4 us
    all_to_all x1, blocking collectives, on_device(): lax.all_to_all(core_rows, MODE, split_axis=0, concat_axis=0, tiled=True)  10.1 us
    ppermute x1, starting transfers between devices, on_device(): twin_gram = lax.ppermute(own_gram, 'core', swap)  9.73 us
    ppermute x1, starting transfers between devices, on_device(): twin = lax.ppermute(own, 'core', swap)  4.92 us
  transfers between devices with their start and end apart: 2, of which 2 were waited for; matrix products, arithmetic and copies ran while one was open for 0% of the time, Pallas kernels for 0%

profile of v7, /device:TPU:1, one launch (start us, length us, event | category | flops | bytes accessed | tf_op | source)
XLA Modules:
  0.0 143.9 jit_solution(6264257832409306947)
XLA Ops:
  0.6 0.0 copy-start
  0.6 1.1 copy.8
  1.7 16.9 %all_to_all.20 = bf16[16,64,256]{2,1,0:T(8,128)(2,1)S(1)} all-to-all(bf16[16,64,256]{2,1,0:T(8,128)(2,1)S(1)} %bitcast.29), channel_id=1, replica_groups=mesh['y'=4,'x'=4,'zh'=4,'z1'=2,'z0'=2,'core'=2] {'y','x'}, dimensions={0} | all-to-all | bytes 1048576 | tf_op jit(solution)/shard_map/all_to_all | solution.py:237
  18.6 4.9 %collective-permute-start = (bf16[1024,256]{1,0:T(8,128)(2,1)S(1)}, bf16[1024,256]{1,0:T(8,128)(2,1)S(1)}, u32[]{:S(2)}, u32[]{:S(2)}) collective-permute-start(bf16[1024,256]{1,0:T(8,128)(2,1)S(1)} %bitcast.25), channel_id=1, source_target_pairs={{0,1},{1,0},{2,3},{3,2},{4,5},{5,4},{6,7},{7,6},{8,9},{9,8},{10,11... | collective-permute-start | bytes 1572872 | tf_op jit(solution)/shard_map/ppermute | solution.py:238
  23.6 0.1 pad_add_fusion.place_ref
  23.6 1.4 collective-permute-done.twin_ref
  25.1 0.0 copy-done
  25.1 1.4 gram.1
  26.5 0.1 convert_element_type.4
  26.6 15.4 %all_to_all.21 = f16[32,80,128]{2,1,0:T(8,128)(2,1)S(1)} all-to-all(f16[32,80,128]{2,1,0:T(8,128)(2,1)S(1)} %bitcast.28), channel_id=1, replica_groups=mesh['y'=4,'x'=4,'zh'=4,'z1'=2,'z0'=2,'core'=2] {'z0','y','x'}, dimensions={0} | all-to-all | bytes 1310720 | tf_op jit(solution)/shard_map/all_to_all | solution.py:252
  42.0 0.1 bitcast_convert_fusion
  42.1 0.1 fusion
  42.2 5.0 %all-gather = f32[18,8,128]{2,1,0:T(8,128)S(1)} all-gather(f32[9,8,128]{2,1,0:T(8,128)S(1)} %fusion), channel_id=2, replica_groups=mesh['y'=4,'x'=4,'zh'=4,'z1'=2,'z0'=2,'core'=2] {'z1'}, dimensions={0}, use_global_device_ids=true | all-gather | bytes 110592 | tf_op jit(solution)/shard_map/all_gather | solution.py:256
  47.2 22.0 %all-gather.1 = f32[36,8,128]{2,1,0:T(8,128)S(1)} all-gather(f32[9,8,128]{2,1,0:T(8,128)S(1)} %reduce_sum.28), channel_id=3, replica_groups=mesh['y'=4,'x'=4,'zh'=4,'z1'=2,'z0'=2,'core'=2] {'zh'}, dimensions={0}, use_global_device_ids=true | all-gather | bytes 184320 | tf_op jit(solution)/shard_map/all_gather | solution.py:256
  69.2 0.1 broadcast_in_dim.2
  69.3 20.1 %all_to_all.22 = f32[32,11,8,128]{3,2,1,0:T(8,128)S(1)} all-to-all(f32[32,11,8,128]{3,2,1,0:T(8,128)S(1)} %broadcast_in_dim.2), channel_id=1, replica_groups=mesh['y'=4,'x'=4,'zh'=4,'z1'=2,'z0'=2,'core'=2] {'z0','y','x'}, dimensions={0} | all-to-all | bytes 2883584 | tf_op jit(solution)/shard_map/all_to_all | solution.py:259
  89.4 9.7 %collective-permute-start.1 = (f32[2,16,11,8,128]{4,3,2,1,0:T(8,128)S(1)}, f32[2,16,11,8,128]{4,3,2,1,0:T(8,128)S(1)}, u32[]{:S(2)}, u32[]{:S(2)}) collective-permute-start(f32[2,16,11,8,128]{4,3,2,1,0:T(8,128)S(1)} %bitcast.23), channel_id=1, source_target_pairs={{0,1},{1,0},{2,3},{3,2},{4,5},{5,4},{6,7},{7,6},{8,9},{9,8},{10,11... | collective-permute-start | bytes 4325384 | tf_op jit(solution)/shard_map/ppermute | solution.py:261
  99.1 2.6 %collective-permute-done.1.twin_ref = f32[2,16,11,8,128]{4,3,2,1,0:T(8,128)S(1)} collective-permute-done((f32[2,16,11,8,128]{4,3,2,1,0:T(8,128)S(1)}, f32[2,16,11,8,128]{4,3,2,1,0:T(8,128)S(1)}, u32[]{:S(2)}, u32[]{:S(2)}) %collective-permute-start.1) | collective-permute-done | bytes 1441824 | tf_op jit(solution)/shard_map/ppermute | solution.py:261
  101.8 31.4 %iterate.1 = (f32[64,128]{1,0:T(8,128)}, f32[16,8,256]{2,1,0:T(8,128)S(1)}) custom-call(s32[3]{0:T(128)S(1)} %pad_add_fusion.place_ref, f32[2,16,11,8,128]{4,3,2,1,0:T(8,128)S(1)} %bitcast.24, f32[2,16,11,8,128]{4,3,2,1,0:T(8,128)S(1)} %collective-permute-done.1.twin_ref, bf16[1024,256]{1,0:T(8,128)(2,1)S(1)} %bitcast.27), custom_call_target="tpu_custom_call" | custom-call | tf_op jit(solution)/shard_map/iterate/pallas_call | solution.py:263
  133.2 10.1 %all_to_all.23 = f32[16,8,256]{2,1,0:T(8,128)S(1)} all-to-all(f32[16,8,256]{2,1,0:T(8,128)S(1)} %get-tuple-element.9), channel_id=1, replica_groups=mesh['y'=4,'x'=4,'zh'=4,'z1'=2,'z0'=2,'core'=2] {'y','x'}, dimensions={0} | all-to-all | bytes 262144 | tf_op jit(solution)/shard_map/all_to_all | solution.py:281
  143.3 0.7 copy.10
  (4 shorter events, 0.1 us)
Async XLA Ops:
  0.6 24.4 %copy-start = (f32[64,128]{1,0:T(8,128)S(1)}, f32[64,128]{1,0:T(8,128)}, u32[]{:S(2)}) copy-start(f32[64,128]{1,0:T(8,128)} %initial_ref.1) | copy-start | bytes 98308
  18.6 6.4 %collective-permute-start = (bf16[1024,256]{1,0:T(8,128)(2,1)S(1)}, bf16[1024,256]{1,0:T(8,128)(2,1)S(1)}, u32[]{:S(2)}, u32[]{:S(2)}) collective-permute-start(bf16[1024,256]{1,0:T(8,128)(2,1)S(1)} %bitcast.25), channel_id=1, source_target_pairs={{0,1},{1,0},{2,3},{3,2},{4,5},{5,4},{6,7},{7,6},{8,9},{9,8},{10,11... | collective-permute-start | bytes 1572872 | tf_op jit(solution)/shard_map/ppermute | solution.py:238
  89.4 12.4 %collective-permute-start.1 = (f32[2,16,11,8,128]{4,3,2,1,0:T(8,128)S(1)}, f32[2,16,11,8,128]{4,3,2,1,0:T(8,128)S(1)}, u32[]{:S(2)}, u32[]{:S(2)}) collective-permute-start(f32[2,16,11,8,128]{4,3,2,1,0:T(8,128)S(1)} %bitcast.23), channel_id=1, source_target_pairs={{0,1},{1,0},{2,3},{3,2},{4,5},{5,4},{6,7},{7,6},{8,9},{9,8},{10,11... | collective-permute-start | bytes 4325384 | tf_op jit(solution)/shard_map/ppermute | solution.py:261

commit v8 on v7

--- a/solution.py
+++ b/solution.py
@@ -14,8 +14,8 @@
 SLIVER = BLOCK // SPLIT
 LEAST_PIVOT = 5e-3
 CHUNK = 256
-MODE = ("y", "x")
-PLANES = ("z0", "y", "x")
+MODE = ("x", "y")
+PLANES = ("z0", "x", "y")
 PAIR = HALF_BLOCKS // 2
 SHARE = ROWS // SPLIT // 4
 HALF_TOP = 14.0
@@ -222,7 +222,10 @@
     for half in range(2):
         offset = pl.multiple_of(lax.rem(core * 512 + half * 512, ROWS), 512)
         total = total + dot_tn(pair_ref[0, pl.ds(half * 512, 512), :RANK], field_ref[pl.ds(offset, 512), :])
-    core_ref[...] = total.reshape(core_ref.shape)
+    total = total.reshape(core_ref.shape)
+    for x in range(4):
+        for y in range(4):
+            core_ref[4 * x + y] = total[4 * y + x]
 
 
 def on_device(unfolded, initial):
@@ -284,7 +287,8 @@
 
 def solution(mesh):
     chips = Mesh(mesh.devices.reshape(4, 4, mesh.devices.shape[1] // 8, 2, 2, 2), ("y", "x", "zh", "z1", "z0", "core"))
+    mode = ("y", "x")
     rest = ("zh", "z1", "z0", "core")
-    in_specs = (P(MODE, rest), P(MODE, None))
-    out_specs = (P(MODE, None), P(MODE, rest))
+    in_specs = (P(mode, rest), P(mode, None))
+    out_specs = (P(mode, None), P(mode, rest))
     return jax.shard_map(on_device, mesh=chips, in_specs=in_specs, out_specs=out_specs, check_vma=False)

time: 144 us -> 144 us (level)
  no operation moved by 1% of the time
where the time goes in v8:
time: 144 us
  blocking collectives  90 us (62%)
  Pallas kernels  32.8 us (23%)
  starting transfers between devices  14.1 us (10%)
  waiting for transfers between devices  4.07 us (3%)
  local copies, waits for them, and re-layouts  1.85 us (1%)
    pallas_call x1, Pallas kernels, on_device(): pl.pallas_call(iterate_kernel, out_shape=(jax.ShapeDtypeStruct((held, RAN...  31.4 us
    all_gather x2, blocking collectives, on_device(): sliver = jnp.sum(lax.all_gather(sliver, axis, axis=0, tiled=False), axis=0)  26.7 us
    all_to_all x1, blocking collectives, on_device(): lax.all_to_all(got, PLANES, split_axis=0, concat_axis=0, tiled=True)  20.8 us
    all_to_all x1, blocking collectives, on_device(): lax.all_to_all(parts, MODE, split_axis=0, concat_axis=0, tiled=True)  16.6 us
    all_to_all x1, blocking collectives, on_device(): lax.all_to_all(partial_gram, PLANES, split_axis=0, concat_axis=0, tiled=T...  16 us
    all_to_all x1, blocking collectives, on_device(): lax.all_to_all(core_rows, MODE, split_axis=0, concat_axis=0, tiled=True)  9.88 us
    ppermute x1, starting transfers between devices, on_device(): twin_gram = lax.ppermute(own_gram, 'core', swap)  8.97 us
    ppermute x1, starting transfers between devices, on_device(): twin = lax.ppermute(own, 'core', swap)  5.13 us
  transfers between devices with their start and end apart: 2, of which 2 were waited for; matrix products, arithmetic and copies ran while one was open for 0% of the time, Pallas kernels for 0%

profile of v8, /device:TPU:1, one launch (start us, length us, event | category | flops | bytes accessed | tf_op | source)
XLA Modules:
  0.0 143.9 jit_solution(17561608962470048398)
XLA Ops:
  0.6 0.0 copy-start
  0.6 1.1 copy.8
  1.7 16.6 %all_to_all.20 = bf16[16,64,256]{2,1,0:T(8,128)(2,1)S(1)} all-to-all(bf16[16,64,256]{2,1,0:T(8,128)(2,1)S(1)} %bitcast.29), channel_id=1, replica_groups=mesh['y'=4,'x'=4,'zh'=4,'z1'=2,'z0'=2,'core'=2] {'x','y'}, dimensions={0} | all-to-all | bytes 1048576 | tf_op jit(solution)/shard_map/all_to_all | solution.py:240
  18.3 5.1 %collective-permute-start = (bf16[1024,256]{1,0:T(8,128)(2,1)S(1)}, bf16[1024,256]{1,0:T(8,128)(2,1)S(1)}, u32[]{:S(2)}, u32[]{:S(2)}) collective-permute-start(bf16[1024,256]{1,0:T(8,128)(2,1)S(1)} %bitcast.25), channel_id=1, source_target_pairs={{0,1},{1,0},{2,3},{3,2},{4,5},{5,4},{6,7},{7,6},{8,9},{9,8},{10,11... | collective-permute-start | bytes 1572872 | tf_op jit(solution)/shard_map/ppermute | solution.py:241
  23.5 0.1 pad_add_fusion.place_ref
  23.6 1.4 collective-permute-done.twin_ref
  25.0 0.0 copy-done
  25.0 1.4 gram.1
  26.4 0.1 convert_element_type.4
  26.5 16.0 %all_to_all.21 = f16[32,80,128]{2,1,0:T(8,128)(2,1)S(1)} all-to-all(f16[32,80,128]{2,1,0:T(8,128)(2,1)S(1)} %bitcast.28), channel_id=1, replica_groups=mesh['y'=4,'x'=4,'zh'=4,'z1'=2,'z0'=2,'core'=2] {'z0','x','y'}, dimensions={0} | all-to-all | bytes 1310720 | tf_op jit(solution)/shard_map/all_to_all | solution.py:255
  42.4 0.1 bitcast_convert_fusion
  42.6 0.1 fusion
  42.7 5.0 %all-gather = f32[18,8,128]{2,1,0:T(8,128)S(1)} all-gather(f32[9,8,128]{2,1,0:T(8,128)S(1)} %fusion), channel_id=2, replica_groups=mesh['y'=4,'x'=4,'zh'=4,'z1'=2,'z0'=2,'core'=2] {'z1'}, dimensions={0}, use_global_device_ids=true | all-gather | bytes 110592 | tf_op jit(solution)/shard_map/all_gather | solution.py:259
  47.7 21.7 %all-gather.1 = f32[36,8,128]{2,1,0:T(8,128)S(1)} all-gather(f32[9,8,128]{2,1,0:T(8,128)S(1)} %reduce_sum.28), channel_id=3, replica_groups=mesh['y'=4,'x'=4,'zh'=4,'z1'=2,'z0'=2,'core'=2] {'zh'}, dimensions={0}, use_global_device_ids=true | all-gather | bytes 184320 | tf_op jit(solution)/shard_map/all_gather | solution.py:259
  69.4 0.1 broadcast_in_dim.2
  69.5 20.8 %all_to_all.22 = f32[32,11,8,128]{3,2,1,0:T(8,128)S(1)} all-to-all(f32[32,11,8,128]{3,2,1,0:T(8,128)S(1)} %broadcast_in_dim.2), channel_id=1, replica_groups=mesh['y'=4,'x'=4,'zh'=4,'z1'=2,'z0'=2,'core'=2] {'z0','x','y'}, dimensions={0} | all-to-all | bytes 2883584 | tf_op jit(solution)/shard_map/all_to_all | solution.py:262
  90.3 9.0 %collective-permute-start.1 = (f32[2,16,11,8,128]{4,3,2,1,0:T(8,128)S(1)}, f32[2,16,11,8,128]{4,3,2,1,0:T(8,128)S(1)}, u32[]{:S(2)}, u32[]{:S(2)}) collective-permute-start(f32[2,16,11,8,128]{4,3,2,1,0:T(8,128)S(1)} %bitcast.23), channel_id=1, source_target_pairs={{0,1},{1,0},{2,3},{3,2},{4,5},{5,4},{6,7},{7,6},{8,9},{9,8},{10,11... | collective-permute-start | bytes 4325384 | tf_op jit(solution)/shard_map/ppermute | solution.py:264
  99.3 2.6 %collective-permute-done.1.twin_ref = f32[2,16,11,8,128]{4,3,2,1,0:T(8,128)S(1)} collective-permute-done((f32[2,16,11,8,128]{4,3,2,1,0:T(8,128)S(1)}, f32[2,16,11,8,128]{4,3,2,1,0:T(8,128)S(1)}, u32[]{:S(2)}, u32[]{:S(2)}) %collective-permute-start.1) | collective-permute-done | bytes 1441824 | tf_op jit(solution)/shard_map/ppermute | solution.py:264
  102.0 31.4 %iterate.1 = (f32[64,128]{1,0:T(8,128)}, f32[16,8,256]{2,1,0:T(8,128)S(1)}) custom-call(s32[3]{0:T(128)S(1)} %pad_add_fusion.place_ref, f32[2,16,11,8,128]{4,3,2,1,0:T(8,128)S(1)} %bitcast.24, f32[2,16,11,8,128]{4,3,2,1,0:T(8,128)S(1)} %collective-permute-done.1.twin_ref, bf16[1024,256]{1,0:T(8,128)(2,1)S(1)} %bitcast.27), custom_call_target="tpu_custom_call" | custom-call | tf_op jit(solution)/shard_map/iterate/pallas_call | solution.py:266
  133.4 9.9 %all_to_all.23 = f32[16,8,256]{2,1,0:T(8,128)S(1)} all-to-all(f32[16,8,256]{2,1,0:T(8,128)S(1)} %get-tuple-element.9), channel_id=1, replica_groups=mesh['y'=4,'x'=4,'zh'=4,'z1'=2,'z0'=2,'core'=2] {'x','y'}, dimensions={0} | all-to-all | bytes 262144 | tf_op jit(solution)/shard_map/all_to_all | solution.py:284
  143.3 0.7 copy.10
  (4 shorter events, 0.1 us)
Async XLA Ops:
  0.6 24.4 %copy-start = (f32[64,128]{1,0:T(8,128)S(1)}, f32[64,128]{1,0:T(8,128)}, u32[]{:S(2)}) copy-start(f32[64,128]{1,0:T(8,128)} %initial_ref.1) | copy-start | bytes 98308
  18.3 6.7 %collective-permute-start = (bf16[1024,256]{1,0:T(8,128)(2,1)S(1)}, bf16[1024,256]{1,0:T(8,128)(2,1)S(1)}, u32[]{:S(2)}, u32[]{:S(2)}) collective-permute-start(bf16[1024,256]{1,0:T(8,128)(2,1)S(1)} %bitcast.25), channel_id=1, source_target_pairs={{0,1},{1,0},{2,3},{3,2},{4,5},{5,4},{6,7},{7,6},{8,9},{9,8},{10,11... | collective-permute-start | bytes 1572872 | tf_op jit(solution)/shard_map/ppermute | solution.py:241
  90.3 11.6 %collective-permute-start.1 = (f32[2,16,11,8,128]{4,3,2,1,0:T(8,128)S(1)}, f32[2,16,11,8,128]{4,3,2,1,0:T(8,128)S(1)}, u32[]{:S(2)}, u32[]{:S(2)}) collective-permute-start(f32[2,16,11,8,128]{4,3,2,1,0:T(8,128)S(1)} %bitcast.23), channel_id=1, source_target_pairs={{0,1},{1,0},{2,3},{3,2},{4,5},{5,4},{6,7},{7,6},{8,9},{9,8},{10,11... | collective-permute-start | bytes 4325384 | tf_op jit(solution)/shard_map/ppermute | solution.py:264

commit v9 on v8

--- a/solution.py
+++ b/solution.py
@@ -255,7 +255,7 @@
     got = lax.all_to_all(partial_gram, PLANES, split_axis=0, concat_axis=0, tiled=True)
     got = got.astype(jnp.float32).reshape(2 * SPLIT, PAIR + 1, SLIVER, BLOCK)
     sliver = jnp.sum(got[:, :PAIR] * jnp.exp2(got[:, PAIR:] - HALF_TOP), axis=0)
-    for axis in ("z1", "zh"):
+    for axis in ("zh", "z1"):
         sliver = jnp.sum(lax.all_gather(sliver, axis, axis=0, tiled=False), axis=0)
     sliver = jnp.concatenate([sliver, share], axis=0)
     got = jnp.broadcast_to(sliver[None], (2 * SPLIT,) + sliver.shape)

time: 144 us -> 144 us (level)
  no operation moved by 1% of the time
where the time goes in v9:
time: 144 us
  blocking collectives  90 us (62%)
  Pallas kernels  32.8 us (23%)
  starting transfers between devices  13.7 us (10%)
  waiting for transfers between devices  4.07 us (3%)
  local copies, waits for them, and re-layouts  1.85 us (1%)
    pallas_call x1, Pallas kernels, on_device(): pl.pallas_call(iterate_kernel, out_shape=(jax.ShapeDtypeStruct((held, RAN...  31.4 us
    all_gather x2, blocking collectives, on_device(): sliver = jnp.sum(lax.all_gather(sliver, axis, axis=0, tiled=False), axis=0)  27 us
    all_to_all x1, blocking collectives, on_device(): lax.all_to_all(got, PLANES, split_axis=0, concat_axis=0, tiled=True)  20.5 us
    all_to_all x1, blocking collectives, on_device(): lax.all_to_all(parts, MODE, split_axis=0, concat_axis=0, tiled=True)  16.6 us
    all_to_all x1, blocking collectives, on_device(): lax.all_to_all(partial_gram, PLANES, split_axis=0, concat_axis=0, tiled=T...  16 us
    all_to_all x1, blocking collectives, on_device(): lax.all_to_all(core_rows, MODE, split_axis=0, concat_axis=0, tiled=True)  9.86 us
    ppermute x1, starting transfers between devices, on_device(): twin_gram = lax.ppermute(own_gram, 'core', swap)  8.59 us
    ppermute x1, starting transfers between devices, on_device(): twin = lax.ppermute(own, 'core', swap)  5.13 us
  transfers between devices with their start and end apart: 2, of which 2 were waited for; matrix products, arithmetic and copies ran while one was open for 0% of the time, Pallas kernels for 0%

profile of v9, /device:TPU:1, one launch (start us, length us, event | category | flops | bytes accessed | tf_op | source)
XLA Modules:
  0.0 143.6 jit_solution(4946461827224514298)
XLA Ops:
  0.6 0.0 copy-start
  0.6 1.1 copy.8
  1.7 16.6 %all_to_all.20 = bf16[16,64,256]{2,1,0:T(8,128)(2,1)S(1)} all-to-all(bf16[16,64,256]{2,1,0:T(8,128)(2,1)S(1)} %bitcast.29), channel_id=1, replica_groups=mesh['y'=4,'x'=4,'zh'=4,'z1'=2,'z0'=2,'core'=2] {'x','y'}, dimensions={0} | all-to-all | bytes 1048576 | tf_op jit(solution)/shard_map/all_to_all | solution.py:240
  18.3 5.1 %collective-permute-start = (bf16[1024,256]{1,0:T(8,128)(2,1)S(1)}, bf16[1024,256]{1,0:T(8,128)(2,1)S(1)}, u32[]{:S(2)}, u32[]{:S(2)}) collective-permute-start(bf16[1024,256]{1,0:T(8,128)(2,1)S(1)} %bitcast.25), channel_id=1, source_target_pairs={{0,1},{1,0},{2,3},{3,2},{4,5},{5,4},{6,7},{7,6},{8,9},{9,8},{10,11... | collective-permute-start | bytes 1572872 | tf_op jit(solution)/shard_map/ppermute | solution.py:241
  23.5 0.1 pad_add_fusion.place_ref
  23.6 1.4 collective-permute-done.twin_ref
  25.0 0.0 copy-done
  25.0 1.4 gram.1
  26.4 0.1 convert_element_type.4
  26.5 16.0 %all_to_all.21 = f16[32,80,128]{2,1,0:T(8,128)(2,1)S(1)} all-to-all(f16[32,80,128]{2,1,0:T(8,128)(2,1)S(1)} %bitcast.28), channel_id=1, replica_groups=mesh['y'=4,'x'=4,'zh'=4,'z1'=2,'z0'=2,'core'=2] {'z0','x','y'}, dimensions={0} | all-to-all | bytes 1310720 | tf_op jit(solution)/shard_map/all_to_all | solution.py:255
  42.4 0.1 bitcast_convert_fusion
  42.6 0.1 fusion
  42.7 22.6 %all-gather = f32[36,8,128]{2,1,0:T(8,128)S(1)} all-gather(f32[9,8,128]{2,1,0:T(8,128)S(1)} %fusion), channel_id=2, replica_groups=mesh['y'=4,'x'=4,'zh'=4,'z1'=2,'z0'=2,'core'=2] {'zh'}, dimensions={0}, use_global_device_ids=true | all-gather | bytes 184320 | tf_op jit(solution)/shard_map/all_gather | solution.py:259
  65.3 4.4 %all-gather.1 = f32[18,8,128]{2,1,0:T(8,128)S(1)} all-gather(f32[9,8,128]{2,1,0:T(8,128)S(1)} %reduce_sum.28), channel_id=3, replica_groups=mesh['y'=4,'x'=4,'zh'=4,'z1'=2,'z0'=2,'core'=2] {'z1'}, dimensions={0}, use_global_device_ids=true | all-gather | bytes 110592 | tf_op jit(solution)/shard_map/all_gather | solution.py:259
  69.7 0.1 broadcast_in_dim.2
  69.9 20.5 %all_to_all.22 = f32[32,11,8,128]{3,2,1,0:T(8,128)S(1)} all-to-all(f32[32,11,8,128]{3,2,1,0:T(8,128)S(1)} %broadcast_in_dim.2), channel_id=1, replica_groups=mesh['y'=4,'x'=4,'zh'=4,'z1'=2,'z0'=2,'core'=2] {'z0','x','y'}, dimensions={0} | all-to-all | bytes 2883584 | tf_op jit(solution)/shard_map/all_to_all | solution.py:262
  90.4 8.6 %collective-permute-start.1 = (f32[2,16,11,8,128]{4,3,2,1,0:T(8,128)S(1)}, f32[2,16,11,8,128]{4,3,2,1,0:T(8,128)S(1)}, u32[]{:S(2)}, u32[]{:S(2)}) collective-permute-start(f32[2,16,11,8,128]{4,3,2,1,0:T(8,128)S(1)} %bitcast.23), channel_id=1, source_target_pairs={{0,1},{1,0},{2,3},{3,2},{4,5},{5,4},{6,7},{7,6},{8,9},{9,8},{10,11... | collective-permute-start | bytes 4325384 | tf_op jit(solution)/shard_map/ppermute | solution.py:264
  99.0 2.6 %collective-permute-done.1.twin_ref = f32[2,16,11,8,128]{4,3,2,1,0:T(8,128)S(1)} collective-permute-done((f32[2,16,11,8,128]{4,3,2,1,0:T(8,128)S(1)}, f32[2,16,11,8,128]{4,3,2,1,0:T(8,128)S(1)}, u32[]{:S(2)}, u32[]{:S(2)}) %collective-permute-start.1) | collective-permute-done | bytes 1441824 | tf_op jit(solution)/shard_map/ppermute | solution.py:264
  101.6 31.4 %iterate.1 = (f32[64,128]{1,0:T(8,128)}, f32[16,8,256]{2,1,0:T(8,128)S(1)}) custom-call(s32[3]{0:T(128)S(1)} %pad_add_fusion.place_ref, f32[2,16,11,8,128]{4,3,2,1,0:T(8,128)S(1)} %bitcast.24, f32[2,16,11,8,128]{4,3,2,1,0:T(8,128)S(1)} %collective-permute-done.1.twin_ref, bf16[1024,256]{1,0:T(8,128)(2,1)S(1)} %bitcast.27), custom_call_target="tpu_custom_call" | custom-call | tf_op jit(solution)/shard_map/iterate/pallas_call | solution.py:266
  133.0 9.9 %all_to_all.23 = f32[16,8,256]{2,1,0:T(8,128)S(1)} all-to-all(f32[16,8,256]{2,1,0:T(8,128)S(1)} %get-tuple-element.9), channel_id=1, replica_groups=mesh['y'=4,'x'=4,'zh'=4,'z1'=2,'z0'=2,'core'=2] {'x','y'}, dimensions={0} | all-to-all | bytes 262144 | tf_op jit(solution)/shard_map/all_to_all | solution.py:284
  142.9 0.7 copy.10
  (4 shorter events, 0.1 us)
Async XLA Ops:
  0.6 24.4 %copy-start = (f32[64,128]{1,0:T(8,128)S(1)}, f32[64,128]{1,0:T(8,128)}, u32[]{:S(2)}) copy-start(f32[64,128]{1,0:T(8,128)} %initial_ref.1) | copy-start | bytes 98308
  18.3 6.7 %collective-permute-start = (bf16[1024,256]{1,0:T(8,128)(2,1)S(1)}, bf16[1024,256]{1,0:T(8,128)(2,1)S(1)}, u32[]{:S(2)}, u32[]{:S(2)}) collective-permute-start(bf16[1024,256]{1,0:T(8,128)(2,1)S(1)} %bitcast.25), channel_id=1, source_target_pairs={{0,1},{1,0},{2,3},{3,2},{4,5},{5,4},{6,7},{7,6},{8,9},{9,8},{10,11... | collective-permute-start | bytes 1572872 | tf_op jit(solution)/shard_map/ppermute | solution.py:241
  90.4 11.2 %collective-permute-start.1 = (f32[2,16,11,8,128]{4,3,2,1,0:T(8,128)S(1)}, f32[2,16,11,8,128]{4,3,2,1,0:T(8,128)S(1)}, u32[]{:S(2)}, u32[]{:S(2)}) collective-permute-start(f32[2,16,11,8,128]{4,3,2,1,0:T(8,128)S(1)} %bitcast.23), channel_id=1, source_target_pairs={{0,1},{1,0},{2,3},{3,2},{4,5},{5,4},{6,7},{7,6},{8,9},{9,8},{10,11... | collective-permute-start | bytes 4325384 | tf_op jit(solution)/shard_map/ppermute | solution.py:264
